TPU v7x, 128 devices: a whole 4x4x4 slice. The times are simulated.
128 devices in a mesh: grp: 4 (over z), head: 32 (over y, x, core).
Axes of the slice: x: 4, y: 4, z: 4, core: 2. Of those that a mesh axis runs over, the one named last changes fastest.
Arguments:
- prompt: bfloat16 [49152, 7168], P(('grp', 'head')), may hold values from -6 to 6
- w_dkv: bfloat16 [7168, 576], replicated, may hold values from -0.0625 to 0.0625
- kv_gain: float32 [512], replicated, may hold values from 0.1 to 1.9
- block_table: int32 [128, 16], replicated, may hold values from 0 to 767, as said below
- ctx_pages: int32 [128], replicated, may hold values from 1 to 16, as said below
- dec_hidden: bfloat16 [128, 2, 7168], P('grp'), may hold values from -6 to 6
- w_dq: bfloat16 [7168, 1536], P('head'), may hold values from -0.0625 to 0.0625
- q_gain: float32 [1536], replicated, may hold values from 0.1 to 1.9
- w_uq: bfloat16 [1536, 24576], P(None, 'head'), may hold values from -0.15625 to 0.15625
- w_uk: bfloat16 [128, 128, 512], P('head')
- w_uv: bfloat16 [128, 512, 128], P('head'), may hold values from -0.25 to 0.25
- w_o: bfloat16 [16384, 7168], P('head'), may hold values from -0.09375 to 0.09375
Outputs:
- attn_out: bfloat16 [128, 2, 7168], P('grp', None, 'head')
Inputs may be any that keep to these rules, and one draw needn't show every extreme that they name: `block_table`: request r * 32 + q belongs to decode rank r. The first ctx_pages[q] entries of row q are that request's pages in order; over all requests they name every page id exactly once. Entries past ctx_pages[q] are arbitrary page ids. Page n was prefilled by device n // 6 (grp index times 32 plus head index); at most 3 pages of one prefill device belong to one decode rank, and every prefill device has 3 pages for some rank. `ctx_pages`: the lengths of one rank's requests sum to the number of pages that rank receives; some request has 16 pages in every draw.
All inputs are finite; a program needn't handle non-finite values.
Results may differ from a plain program's by a relative error of at most 0.039.
Values may be sent and summed in bfloat16 or wider, within the bound.
A program may use at most 192 MiB of HBM per device.

v0:
```python
import jax
import jax.numpy as jnp
from jax import lax
from jax.experimental import pallas as pl
from jax.experimental.pallas import tpu as pltpu
from jax.sharding import PartitionSpec as P

PAGE = 64
SLOT = 3
MAXP = 16
LAT = 512
ROPE = 64
NOPE = 128
QL = 1536
NH = 4
NG = 4
NY = 4
NB = 8
N_HEAD = 32
ROWS = SLOT * PAGE
RROWS = SLOT * PAGE // 2
KCHUNK = 1024
OFFS = (0, 1, 3, 2)
MESH = pl.DeviceIdType.MESH
F32 = jnp.float32
BF16 = jnp.bfloat16
LOW = -1e30


def dot(a, b):
    return jnp.dot(a, b, preferred_element_type=F32)


def dot_t(a, b):
    return lax.dot_general(a, b, (((1,), (1,)), ((), ())), preferred_element_type=F32)


def norm_rows(values, gain_row, width):
    mean = jnp.sum(values * values, axis=-1, keepdims=True) * (1.0 / width)
    return values * lax.rsqrt(mean + 1e-06) * gain_row


def rotate_pairs(x, cosine, signed_sine):
    lane = lax.broadcasted_iota(jnp.int32, x.shape, 1)
    swapped = jnp.where((lane & 63) < 32, pltpu.roll(x, 96, 1), pltpu.roll(x, 32, 1))
    return x * cosine + swapped * signed_sine


def rows_by_request(transposed):
    i = lax.broadcasted_iota(jnp.int32, (256, 256), 1 if transposed else 0)
    j = lax.broadcasted_iota(jnp.int32, (256, 256), 0 if transposed else 1)
    place = ((i >> 1) & 3) * 64 + (i >> 3) * 2 + (i & 1)
    return jnp.where(j == place, 1.0, 0.0).astype(BF16)


def gather_kernel(
    send_idx,
    hpart,
    w_dq,
    kv_gain,
    q_gain,
    page_cos,
    page_sin,
    new_cos,
    new_sin,
    prompt,
    hidden,
    w_dkv,
    w_uq,
    w_uk,
    lat_all,
    rope_all,
    q_lat,
    q_rope,
    new_lat,
    new_rope,
    pbuf,
    wbuf,
    acc,
    uq_buf,
    uk_buf,
    lat_own,
    rope_own,
    zlat,
    zrope,
    qpart,
    rq_land,
    red,
    qlat,
    qmine,
    qrmine,
    load_sem,
    w_sem,
    own_sem,
    z_send,
    z_recv,
    x_send,
    x_recv,
    f_send,
    f_recv,
    c_send,
    c_recv,
    r_send,
    r_recv,
    g_send,
    g_recv,
    y_send,
    y_recv,
):
    g = lax.axis_index("grp")
    h = lax.axis_index("head")
    y = h // NB
    b = h % NB
    x = b // 2
    c = b % 2
    sibling = h + 1 - 2 * c
    right = y * NB + ((x + 1) % 4) * 2 + c
    left = y * NB + ((x + 3) % 4) * 2 + c
    b_left = ((x + 3) % 4) * 2 + c
    b_right = ((x + 1) % 4) * 2 + c
    b_far = ((x + 2) % 4) * 2 + c

    barrier = pltpu.get_barrier_semaphore()

    @pl.loop(1, N_HEAD)
    def _(o):
        pl.semaphore_signal(
            barrier, inc=1, device_id={"head": (h + o) % N_HEAD}, device_id_type=MESH
        )

    for o in (1, 2, 3):
        pl.semaphore_signal(barrier, inc=1, device_id={"grp": (g + o) % NG}, device_id_type=MESH)

    depth = prompt.shape[1]
    tokens = prompt.shape[0]
    chunks = depth // KCHUNK
    loads = []
    for k in range(chunks):
        cols = pl.ds(k * KCHUNK, KCHUNK)
        loads.append(
            [
                pltpu.make_async_copy(
                    prompt.at[:, cols], pbuf.at[pl.ds(0, tokens), cols], load_sem.at[k, 0]
                ),
                pltpu.make_async_copy(
                    hidden.at[:, cols], pbuf.at[pl.ds(tokens, 64), cols], load_sem.at[k, 1]
                ),
                pltpu.make_async_copy(w_dkv.at[cols, :], wbuf.at[cols, :], load_sem.at[k, 2]),
            ]
        )
    for group in loads:
        for one in group:
            one.start()
    uq_copy = pltpu.make_async_copy(w_uq, uq_buf, w_sem.at[0])
    uk_copy = pltpu.make_async_copy(w_uk, uk_buf, w_sem.at[1])
    uq_copy.start()
    uk_copy.start()

    qpart[...] = dot(hpart[...], w_dq[...])
    pl.semaphore_wait(barrier, N_HEAD - 1 + 3)

    def q_block(i):
        return (
            pl.ds(pl.multiple_of((i // 4) * 8, 8), 8),
            pl.ds(pl.multiple_of((i % 4) * 384, 128), 384),
        )

    def share_copy(to):
        return pltpu.make_async_remote_copy(
            src_ref=qpart.at[q_block(to)],
            dst_ref=rq_land.at[h],
            send_sem=r_send.at[to],
            recv_sem=r_recv.at[h],
            device_id={"head": to},
            device_id_type=MESH,
        )

    @pl.loop(1, N_HEAD)
    def _(o):
        share_copy((h + o) % N_HEAD).start()

    for k in range(chunks):
        for one in loads[k]:
            one.wait()
        part = dot(pbuf[:, k * KCHUNK : (k + 1) * KCHUNK], wbuf[k * KCHUNK : (k + 1) * KCHUNK, :])
        if k == 0:
            acc[...] = part
        else:
            acc[...] += part

    pages = tokens // PAGE
    lat_own[...] = (
        norm_rows(acc[0:tokens, 0:LAT], kv_gain[...], LAT).astype(BF16).reshape(pages, PAGE, LAT)
    )
    halves = []
    for p in range(pages):
        first = acc[p * PAGE : p * PAGE + 32, LAT : LAT + ROPE]
        second = acc[p * PAGE + 32 : p * PAGE + 64, LAT : LAT + ROPE]
        halves.append(jnp.concatenate([first, second], axis=1))
    packed = jnp.concatenate(halves, axis=0)
    rope_own[...] = (
        rotate_pairs(packed, page_cos[...], page_sin[...]).astype(BF16).reshape(pages, 32, 128)
    )

    for j in range(4):
        rank = (g + OFFS[j]) % NG
        for k in range(SLOT):
            page = send_idx[rank * SLOT + k]
            zlat[j, k * PAGE : (k + 1) * PAGE, :] = lat_own[page]
            zrope[j, k * 32 : (k + 1) * 32, :] = rope_own[page]

    def z_copies(j):
        rank = (g + OFFS[j]) % NG
        return [
            pltpu.make_async_remote_copy(
                src_ref=src.at[j],
                dst_ref=dst.at[b, g],
                send_sem=z_send.at[j - 1, i],
                recv_sem=z_recv.at[j - 1, i],
                device_id={"grp": rank},
                device_id_type=MESH,
            )
            for i, (src, dst) in enumerate(((zlat, lat_all), (zrope, rope_all)))
        ]

    def plane(j):
        return (g + NG - OFFS[j]) % NG

    def ring_copies(j, block, to, send_sem, recv_sem):
        gs = plane(j)
        out = []
        for i, (mine, ref) in enumerate(((zlat, lat_all), (zrope, rope_all))):
            src = mine.at[0] if (j == 0 and block is b) else ref.at[block, gs]
            out.append(
                pltpu.make_async_remote_copy(
                    src_ref=src,
                    dst_ref=ref.at[block, gs],
                    send_sem=send_sem.at[i],
                    recv_sem=recv_sem.at[i],
                    device_id={"head": to},
                    device_id_type=MESH,
                )
            )
        return out

    def to_right(j):
        return ring_copies(j, b, right, x_send.at[j, 0], x_recv.at[j, 0])

    def to_left(j):
        return ring_copies(j, b, left, x_send.at[j, 1], x_recv.at[j, 1])

    def onward(j):
        if j in (0, 3):
            return ring_copies(j, b_left, right, f_send.at[j], f_recv.at[j])
        return ring_copies(j, b_right, left, f_send.at[j], f_recv.at[j])

    blocks = (b, b_left, b_right, b_far)

    def across(j, which):
        return ring_copies(j, blocks[which], sibling, c_send.at[j, which], c_recv.at[j, which])

    def start(copies):
        for one in copies:
            one.start()

    def wait_recv(copies):
        for one in copies:
            one.wait_recv()

    def wait_send(copies):
        for one in copies:
            one.wait_send()

    def arrived(ref_block, j, sem):
        gs = plane(j)
        for i, ref in enumerate((lat_all, rope_all)):
            pltpu.make_async_remote_copy(
                src_ref=ref.at[ref_block, gs],
                dst_ref=ref.at[ref_block, gs],
                send_sem=sem.at[i],
                recv_sem=sem.at[i],
                device_id={"head": sibling},
                device_id_type=MESH,
            ).wait_recv()

    def serve_own(j):
        start(to_right(j))
        start(to_left(j))
        start(across(j, 0))

    def serve_near(j):
        arrived(b_left, j, x_recv.at[j, 0])
        if j in (0, 3):
            start(onward(j))
        start(across(j, 1))
        arrived(b_right, j, x_recv.at[j, 1])
        if j in (1, 2):
            start(onward(j))
        start(across(j, 2))

    def serve_far(j):
        arrived(b_far, j, f_recv.at[j])
        start(across(j, 3))

    for j in (1, 2, 3):
        start(z_copies(j))
    own = [
        pltpu.make_async_copy(zlat.at[0], lat_all.at[b, g], own_sem.at[0]),
        pltpu.make_async_copy(zrope.at[0], rope_all.at[b, g], own_sem.at[1]),
    ]
    start(own)
    serve_own(0)

    new_lat[...] = norm_rows(acc[tokens : tokens + 64, 0:LAT], kv_gain[...], LAT).astype(BF16)
    new_r = acc[tokens : tokens + 64, LAT : LAT + ROPE]
    new_r = rotate_pairs(jnp.concatenate([new_r, new_r], axis=1), new_cos[...], new_sin[...])
    lane = lax.broadcasted_iota(jnp.int32, new_r.shape, 1)
    new_rope[...] = jnp.where(lane < ROPE, new_r, 0.0).astype(BF16)

    rq_land[h] = qpart[q_block(h)]

    @pl.loop(1, N_HEAD)
    def _(o):
        src = (h + o) % N_HEAD
        pltpu.make_async_remote_copy(
            src_ref=rq_land.at[src],
            dst_ref=rq_land.at[src],
            send_sem=r_send.at[src],
            recv_sem=r_recv.at[src],
            device_id={"head": src},
            device_id_type=MESH,
        ).wait_recv()

    red[...] = jnp.sum(rq_land[...], axis=0)
    qlat[q_block(h)] = red[...]

    def sum_copy(to):
        return pltpu.make_async_remote_copy(
            src_ref=red,
            dst_ref=qlat.at[q_block(h)],
            send_sem=g_send.at[to],
            recv_sem=g_recv.at[h],
            device_id={"head": to},
            device_id_type=MESH,
        )

    @pl.loop(1, N_HEAD)
    def _(o):
        sum_copy((h + o) % N_HEAD).start()

    def z_arrived(j):
        gs = plane(j)
        for i, ref in enumerate((lat_all, rope_all)):
            pltpu.make_async_remote_copy(
                src_ref=ref.at[b, gs],
                dst_ref=ref.at[b, gs],
                send_sem=z_send.at[j - 1, i],
                recv_sem=z_recv.at[j - 1, i],
                device_id={"grp": gs},
                device_id_type=MESH,
            ).wait_recv()

    for j in (1, 2):
        z_arrived(j)
        serve_own(j)
    serve_near(0)

    @pl.loop(1, N_HEAD)
    def _(o):
        src = (h + o) % N_HEAD
        pltpu.make_async_remote_copy(
            src_ref=red,
            dst_ref=qlat.at[q_block(src)],
            send_sem=g_send.at[src],
            recv_sem=g_recv.at[src],
            device_id={"head": src},
            device_id_type=MESH,
        ).wait_recv()

    uq_copy.wait()
    uk_copy.wait()
    query_norm = norm_rows(qlat[...], q_gain[...], QL).astype(BF16)
    queries = dot(query_norm, uq_buf[...])
    parts = []
    ropes = []
    for n in range(NH):
        at = n * (NOPE + ROPE)
        parts.append(dot(queries[:, at : at + NOPE].astype(BF16), uk_buf[n]).astype(BF16))
        one = queries[:, at + NOPE : at + NOPE + ROPE]
        one = jnp.concatenate([one, one], axis=1)
        ropes.append(rotate_pairs(one, new_cos[...], new_sin[...]).astype(BF16))
    order = rows_by_request(False)
    qmine[...] = dot(order, jnp.concatenate(parts, axis=0)).astype(BF16)
    qrmine[...] = dot(order, jnp.concatenate(ropes, axis=0)).astype(BF16)

    def y_copies(o):
        to = ((y + o) % NY) * NB + b
        return [
            pltpu.make_async_remote_copy(
                src_ref=src,
                dst_ref=dst.at[y],
                send_sem=y_send.at[o - 1, i],
                recv_sem=y_recv.at[o - 1, i],
                device_id={"head": to},
                device_id_type=MESH,
            )
            for i, (src, dst) in enumerate(((qmine, q_lat), (qrmine, q_rope)))
        ]

    for o in (1, 2, 3):
        start(y_copies(o))
    own_q = [
        pltpu.make_async_copy(qmine, q_lat.at[y], own_sem.at[2]),
        pltpu.make_async_copy(qrmine, q_rope.at[y], own_sem.at[3]),
    ]
    start(own_q)

    z_arrived(3)
    serve_own(3)
    serve_near(1)
    serve_near(2)
    serve_far(0)
    serve_near(3)
    serve_far(1)
    serve_far(2)
    serve_far(3)

    sib_blocks = tuple(blk + 1 - 2 * c for blk in blocks)
    for j in range(4):
        for which in range(4):
            arrived(sib_blocks[which], j, c_recv.at[j, which])
    for o in (1, 2, 3):
        src = (y + NY - o) % NY
        for i, ref in enumerate((q_lat, q_rope)):
            pltpu.make_async_remote_copy(
                src_ref=ref.at[src],
                dst_ref=ref.at[src],
                send_sem=y_send.at[o - 1, i],
                recv_sem=y_recv.at[o - 1, i],
                device_id={"head": src * NB + b},
                device_id_type=MESH,
            ).wait_recv()

    for one in own + own_q:
        one.wait()
    for j in (1, 2, 3):
        wait_send(z_copies(j))
    for j in range(4):
        wait_send(to_right(j))
        wait_send(to_left(j))
        wait_send(onward(j))
        for which in range(4):
            wait_send(across(j, which))
    for o in (1, 2, 3):
        wait_send(y_copies(o))

    @pl.loop(1, N_HEAD)
    def _(o):
        to = (h + o) % N_HEAD
        share_copy(to).wait_send()
        sum_copy(to).wait_send()


def attend_kernel(
    order,
    owner,
    count,
    lat,
    rope,
    q_lat,
    q_rope,
    new_lat,
    new_rope,
    out,
    stats,
    qf,
    qb,
    acc,
    m_ref,
    l_ref,
):
    my_y = count[1]
    requests = 32
    scale = (NOPE + ROPE) ** (-0.5)
    for yb in range(NY):
        qf[:, yb * 8 : (yb + 1) * 8, 0:LAT] = q_lat[yb].astype(F32).reshape(requests, 8, LAT)
        qf[:, yb * 8 : (yb + 1) * 8, LAT:] = q_rope[yb].astype(F32).reshape(requests, 8, 128)
    qb[0:requests] = qf[...].astype(BF16)
    qb[requests] = jnp.zeros((32, LAT + 128), BF16)

    group = 8
    for r0 in range(0, requests, group):
        rows = group * 32
        q_rows = qb[r0 : r0 + group].reshape(rows, LAT + 128)
        s = (dot_t(q_rows[:, 0:LAT], new_lat[...]) + dot_t(q_rows[:, LAT:], new_rope[...])) * scale
        i = lax.broadcasted_iota(jnp.int32, s.shape, 0) + r0 * 32
        j = lax.broadcasted_iota(jnp.int32, s.shape, 1)
        live = ((i >> 5) == (j >> 1)) & ((j & 1) <= (i & 1)) & (((i >> 3) & 3) == my_y)
        s = jnp.where(live, s, LOW)
        top = jnp.max(s, axis=1, keepdims=True)
        p = jnp.where(live, jnp.exp(s - top), 0.0)
        total = jnp.sum(p, axis=1, keepdims=True)
        acc[r0 : r0 + group] = dot(p.astype(BF16), new_lat[...]).reshape(group, 32, LAT)
        m_ref[r0 : r0 + group] = jnp.broadcast_to(top, (rows, 128)).reshape(group, 32, 128)
        l_ref[r0 : r0 + group] = jnp.broadcast_to(total, (rows, 128)).reshape(group, 32, 128)
    acc[requests] = jnp.zeros((32, LAT), F32)
    m_ref[requests] = jnp.full((32, 128), LOW, F32)
    l_ref[requests] = jnp.zeros((32, 128), F32)

    UNROLL = 4
    lane = lax.broadcasted_iota(jnp.int32, (32, 128), 1)

    @pl.loop(0, (count[0] + UNROLL - 1) // UNROLL)
    def _(it):
        done = []
        for u in range(UNROLL):
            slot = order[it * UNROLL + u]
            r = owner[it * UNROLL + u]
            keys = lat[pl.ds(pl.multiple_of(slot * PAGE, PAGE), PAGE), :]
            pair = rope[pl.ds(pl.multiple_of(slot * 32, 32), 32), :]
            zero = jnp.zeros_like(pair)
            both = jnp.concatenate(
                [jnp.where(lane < ROPE, pair, zero), jnp.where(lane >= ROPE, pair, zero)], axis=0
            )
            q = qb[r]
            s = (dot_t(q[:, 0:LAT], keys) + dot_t(q[:, LAT:], both)) * scale
            top = jnp.max(s, axis=1, keepdims=True)
            p = jnp.exp(s - top)
            total = jnp.sum(p, axis=1, keepdims=True)
            done.append((r, top, total, dot(p.astype(BF16), keys)))
        for r, top, total, o in done:
            m_old = m_ref[r]
            m_new = jnp.maximum(m_old, top)
            a = jnp.exp(m_old - m_new)
            e = jnp.exp(top - m_new)
            m_ref[r] = m_new
            l_ref[r] = l_ref[r] * a + total * e
            acc[r] = acc[r] * a[:, 0:1] + o * e[:, 0:1]

    for yb in range(NY):
        rows = slice(yb * 8, (yb + 1) * 8)
        total = l_ref[0:requests, rows, :]
        some = total > 0.0
        safe = jnp.where(some, total, 1.0)
        inverse = 1.0 / safe
        mixed = acc[0:requests, rows, :] * inverse[:, :, 0:1]
        out[yb] = mixed.reshape(256, LAT).astype(BF16)
        lse = jnp.where(some, m_ref[0:requests, rows, :] + jnp.log(safe), LOW)
        stats[yb] = jnp.transpose(lse.reshape(256, 128))[0:8, :]


def project_kernel(
    part,
    stats,
    w_uv,
    w_o,
    out,
    o_land,
    s_land,
    t_buf,
    wo_buf,
    vals,
    sbuf,
    rbuf,
    w_sem,
    y_send,
    y_recv,
    o_send,
    o_recv,
):
    h = lax.axis_index("head")
    y = h // NB
    b = h % NB
    barrier = pltpu.get_barrier_semaphore()

    @pl.loop(1, N_HEAD)
    def _(o):
        pl.semaphore_signal(
            barrier, inc=1, device_id={"head": (h + o) % N_HEAD}, device_id_type=MESH
        )

    wo_copy = pltpu.make_async_copy(w_o, wo_buf, w_sem)
    wo_copy.start()
    pl.semaphore_wait(barrier, N_HEAD - 1)

    def y_copies(o):
        ty = (y + o) % NY
        return [
            pltpu.make_async_remote_copy(
                src_ref=src.at[ty],
                dst_ref=dst.at[o - 1],
                send_sem=y_send.at[o - 1, i],
                recv_sem=y_recv.at[o - 1, i],
                device_id={"head": ty * NB + b},
                device_id_type=MESH,
            )
            for i, (src, dst) in enumerate(((part, o_land), (stats, s_land)))
        ]

    for o in (2, 1, 3):
        for one in y_copies(o):
            one.start()

    def column(block):
        t_buf[0:8, :] = block
        return jnp.transpose(t_buf[...])[:, 0:1]

    t_buf[...] = jnp.zeros_like(t_buf)
    lses = [column(stats[y])]
    mixes = [part[y].astype(F32)]
    for o in (1, 3, 2):
        for one in y_copies(o):
            one.wait_recv()
        lses.append(column(s_land[o - 1]))
        mixes.append(o_land[o - 1].astype(F32))
    top = jnp.maximum(jnp.maximum(lses[0], lses[1]), jnp.maximum(lses[2], lses[3]))
    weights = [jnp.exp(one - top) for one in lses]
    total = weights[0] + weights[1] + weights[2] + weights[3]
    mixed = mixes[0] * (weights[0] / total)
    for one, weight in zip(mixes[1:], weights[1:]):
        mixed += one * (weight / total)
    by_head = dot(rows_by_request(True), mixed.astype(BF16)).astype(BF16)
    for n in range(NH):
        vals[:, n * 128 : (n + 1) * 128] = dot(
            by_head[n * 64 : (n + 1) * 64, :], w_uv[n]
        ).astype(BF16)

    def out_copy(to):
        return pltpu.make_async_remote_copy(
            src_ref=sbuf.at[to],
            dst_ref=rbuf.at[h],
            send_sem=o_send.at[to],
            recv_sem=o_recv.at[h],
            device_id={"head": to},
            device_id_type=MESH,
        )

    wo_copy.wait()
    width = out.shape[1]
    span = width * NB
    for i in range(NY):
        ty = (y + i) % NY
        cols = pl.ds(pl.multiple_of(ty * span, 128), span)
        piece = dot(vals[...], wo_buf[:, cols])
        for k in range(NB):
            to = ty * NB + k
            sbuf[to] = piece[:, k * width : (k + 1) * width].astype(BF16)

            @pl.when(to != h)
            def _():
                out_copy(to).start()

    def body(o, total):
        src = (h + o) % N_HEAD
        pltpu.make_async_remote_copy(
            src_ref=rbuf.at[src],
            dst_ref=rbuf.at[src],
            send_sem=o_send.at[src],
            recv_sem=o_recv.at[src],
            device_id={"head": src},
            device_id_type=MESH,
        ).wait_recv()
        return total + rbuf[src].astype(F32)

    result = lax.fori_loop(1, N_HEAD, body, sbuf[h].astype(F32))
    out[...] = result.astype(BF16)

    for o in (1, 2, 3):
        for one in y_copies(o):
            one.wait_send()

    @pl.loop(1, N_HEAD)
    def _(o):
        out_copy((h + o) % N_HEAD).wait_send()


def spec(space):
    return pl.BlockSpec(memory_space=space)


VM, SM, ANY = pltpu.VMEM, pltpu.SMEM, pl.ANY


def page_plan(block_table, ctx_pages, g, y, b, per_rank, pages_dev):
    flat = jnp.where(
        jnp.arange(MAXP, dtype=jnp.int32)[None, :] < ctx_pages[:, None], block_table, -1
    ).reshape(1, -1)
    at = jnp.arange(NG * NB * pages_dev, dtype=jnp.int32)
    per_plane = NB * pages_dev
    ids = (at // per_plane) * (N_HEAD * pages_dev) + y * per_plane + at % per_plane
    codes = jnp.arange(flat.shape[1], dtype=jnp.int32)[None, :]
    code = jnp.sum(jnp.where(flat == ids[:, None], codes, 0), axis=1)
    code = code.reshape(NG, NB, pages_dev)
    target = code // (per_rank * MAXP)
    within = jnp.arange(pages_dev, dtype=jnp.int32)
    alike = (target[..., :, None] == target[..., None, :]) & (within[None, :] < within[:, None])
    slot = jnp.sum(alike.astype(jnp.int32), axis=-1)
    places = jnp.arange(SLOT, dtype=jnp.int32)
    request = (code // MAXP) % per_rank
    here = (target == g)[..., None, :] & (slot[..., None, :] == places[:, None])
    owner = jnp.sum(jnp.where(here, request[..., None, :] + 1, 0), axis=-1) - 1
    owner = owner.transpose(1, 0, 2).reshape(-1)
    mine = lax.dynamic_slice(code, (g, b, 0), (1, 1, pages_dev)).reshape(-1)
    my_target = lax.dynamic_slice(target, (g, b, 0), (1, 1, pages_dev)).reshape(-1)
    my_slot = lax.dynamic_slice(slot, (g, b, 0), (1, 1, pages_dev)).reshape(-1)
    sends = (my_target[None, :] * SLOT + my_slot[None, :]) == jnp.arange(
        NG * SLOT, dtype=jnp.int32
    )[:, None]
    send_idx = jnp.sum(jnp.where(sends, within[None, :], 0), axis=1)
    return owner, send_idx, mine % MAXP


def live_first(owner, spare):
    n = owner.shape[0]
    live = owner >= 0
    before = jnp.arange(n, dtype=jnp.int32)
    rank_live = jnp.sum((live[None, :] & (before[None, :] < before[:, None])).astype(jnp.int32), 1)
    count = jnp.sum(live.astype(jnp.int32))
    place = jnp.where(live, rank_live, count + before - rank_live)
    hit = place[None, :] == before[:, None]
    order = jnp.sum(jnp.where(hit, before[None, :], 0), axis=1)
    owners = jnp.sum(jnp.where(hit, jnp.where(live, owner, spare)[None, :], 0), axis=1)
    return order, owners, count


def angle_tables(positions):
    lane = jnp.arange(2 * ROPE, dtype=jnp.int32)
    inverse_freq = 10000.0 ** (-2.0 * (lane % 32).astype(F32) / ROPE)
    angles = jnp.repeat(positions.astype(F32), ROPE, axis=1) * inverse_freq[None, :]
    sign = jnp.where((lane % ROPE) < 32, -1.0, 1.0).astype(F32)
    return jnp.cos(angles), jnp.sin(angles) * sign[None, :]


def on_device(
    prompt, w_dkv, kv_gain, block_table, ctx_pages, dec_hidden, w_dq, q_gain, w_uq, w_uk, w_uv, w_o
):
    g = lax.axis_index("grp")
    h = lax.axis_index("head")
    y, b = h // NB, h % NB
    tokens, depth = prompt.shape
    pages_dev = tokens // PAGE
    per_rank = dec_hidden.shape[0]
    owner, send_idx, my_depth = page_plan(
        block_table, ctx_pages, g, y, b, per_rank, pages_dev
    )
    order, owners, count = live_first(owner, per_rank)
    lengths = lax.dynamic_slice_in_dim(ctx_pages, g * per_rank, per_rank, 0)
    t = jnp.arange(32, dtype=jnp.int32)
    page_pos = my_depth[:, None, None] * PAGE + t[None, :, None] + jnp.array([0, 32], jnp.int32)
    page_cos, page_sin = angle_tables(page_pos.reshape(-1, 2))
    new_pos = (lengths[:, None] * PAGE + jnp.arange(2, dtype=jnp.int32)[None, :]).reshape(-1, 1)
    new_cos, new_sin = angle_tables(jnp.concatenate([new_pos, new_pos], axis=1))
    hidden = dec_hidden.reshape(per_rank * 2, depth)
    share = w_dq.shape[0]
    hpart = lax.dynamic_slice_in_dim(hidden, h * share, share, 1)

    dma = pltpu.SemaphoreType.DMA
    lat_all, rope_all, q_lat, q_rope, new_lat, new_rope = pl.pallas_call(
        gather_kernel,
        out_shape=[
            jax.ShapeDtypeStruct((NB, NG, ROWS, LAT), BF16),
            jax.ShapeDtypeStruct((NB, NG, RROWS, 128), BF16),
            jax.ShapeDtypeStruct((NY, 256, LAT), BF16),
            jax.ShapeDtypeStruct((NY, 256, 128), BF16),
            jax.ShapeDtypeStruct((64, LAT), BF16),
            jax.ShapeDtypeStruct((64, 128), BF16),
        ],
        in_specs=[spec(SM)] + [spec(VM)] * 8 + [spec(ANY)] * 5,
        out_specs=[spec(ANY)] * 4 + [spec(VM)] * 2,
        scratch_shapes=[
            pltpu.VMEM((tokens + 64, depth), BF16),
            pltpu.VMEM((depth, LAT + ROPE), BF16),
            pltpu.VMEM((tokens + 64, LAT + ROPE), F32),
            pltpu.VMEM(w_uq.shape, BF16),
            pltpu.VMEM(w_uk.shape, BF16),
            pltpu.VMEM((pages_dev, PAGE, LAT), BF16),
            pltpu.VMEM((pages_dev, 32, 128), BF16),
            pltpu.VMEM((NG, ROWS, LAT), BF16),
            pltpu.VMEM((NG, RROWS, 128), BF16),
            pltpu.VMEM((64, QL), F32),
            pltpu.VMEM((N_HEAD, 8, 384), F32),
            pltpu.VMEM((8, 384), F32),
            pltpu.VMEM((64, QL), F32),
            pltpu.VMEM((256, LAT), BF16),
            pltpu.VMEM((256, 128), BF16),
            dma((depth // KCHUNK, 3)),
            dma((2,)),
            dma((4,)),
            dma((3, 2)),
            dma((3, 2)),
            dma((4, 2, 2)),
            dma((4, 2, 2)),
            dma((4, 2)),
            dma((4, 2)),
            dma((4, 4, 2)),
            dma((4, 4, 2)),
            dma((N_HEAD,)),
            dma((N_HEAD,)),
            dma((N_HEAD,)),
            dma((N_HEAD,)),
            dma((3, 2)),
            dma((3, 2)),
        ],
        compiler_params=pltpu.CompilerParams(
            collective_id=0, has_side_effects=True, vmem_limit_bytes=50 * 1024 * 1024
        ),
    )(
        send_idx,
        hpart,
        w_dq,
        kv_gain.reshape(1, -1),
        q_gain.reshape(1, -1),
        page_cos,
        page_sin,
        new_cos,
        new_sin,
        prompt,
        hidden,
        w_dkv,
        w_uq,
        w_uk,
    )

    part, stats = pl.pallas_call(
        attend_kernel,
        out_shape=[
            jax.ShapeDtypeStruct((NY, 256, LAT), BF16),
            jax.ShapeDtypeStruct((NY, 8, 256), F32),
        ],
        in_specs=[spec(SM)] * 3 + [spec(VM)] * 6,
        out_specs=[spec(VM)] * 2,
        scratch_shapes=[
            pltpu.VMEM((32, 32, LAT + 128), F32),
            pltpu.VMEM((33, 32, LAT + 128), BF16),
            pltpu.VMEM((33, 32, LAT), F32),
            pltpu.VMEM((33, 32, 128), F32),
            pltpu.VMEM((33, 32, 128), F32),
        ],
        compiler_params=pltpu.CompilerParams(vmem_limit_bytes=50 * 1024 * 1024),
    )(
        order,
        owners,
        jnp.stack([count, y]),
        lat_all.reshape(-1, LAT),
        rope_all.reshape(-1, 128),
        q_lat,
        q_rope,
        new_lat,
        new_rope,
    )

    width = depth // N_HEAD
    out = pl.pallas_call(
        project_kernel,
        out_shape=jax.ShapeDtypeStruct((64, width), BF16),
        in_specs=[spec(VM)] * 3 + [spec(ANY)],
        out_specs=spec(VM),
        scratch_shapes=[
            pltpu.VMEM((3, 256, LAT), BF16),
            pltpu.VMEM((3, 8, 256), F32),
            pltpu.VMEM((128, 256), F32),
            pltpu.VMEM(w_o.shape, BF16),
            pltpu.VMEM((64, LAT), BF16),
            pltpu.VMEM((N_HEAD, 64, width), BF16),
            pltpu.VMEM((N_HEAD, 64, width), BF16),
            dma(()),
            dma((3, 2)),
            dma((3, 2)),
            dma((N_HEAD,)),
            dma((N_HEAD,)),
        ],
        compiler_params=pltpu.CompilerParams(
            collective_id=1, has_side_effects=True, vmem_limit_bytes=50 * 1024 * 1024
        ),
    )(part, stats, w_uv, w_o)
    return out.reshape(per_rank, 2, width)


def solution(mesh):
    return jax.shard_map(
        on_device,
        mesh=mesh,
        in_specs=(
            P(("grp", "head"), None),
            P(),
            P(),
            P(),
            P(),
            P("grp", None, None),
            P("head", None),
            P(),
            P(None, "head"),
            P("head", None, None),
            P("head", None, None),
            P("head", None),
        ),
        out_specs=P("grp", None, "head"),
        check_vma=False,
    )
```

profile of v0, /device:TPU:1, one launch (start us, length us, event | category | flops | bytes accessed | tf_op | source)
XLA Modules:
  0.0 138.8 jit_solution(4037197907101632016)
XLA Ops:
  0.0 0.7 dynamic-slice_multiply_fusion
  0.8 0.7 reshape.308.q_gain
  1.5 0.7 fusion.6
  2.3 0.1 add.235
  2.5 0.1 broadcast_in_dim.119
  2.7 0.1 sine_multiply_fusion.1
  3.0 0.3 select_reduce_fusion
  3.4 0.1 reshape.304
  3.9 0.1 convert_reduce_fusion
  4.0 0.3 add_reduce_fusion
  4.3 0.7 convert_reduce_fusion.2
  5.1 0.8 pad_add_fusion.count
  6.0 0.1 reshape.305
  6.1 0.1 convert_reduce_fusion.1
  6.3 0.7 subtract_select_fusion
  7.0 0.1 select_reduce_fusion.1
  7.2 0.4 sine_multiply_fusion
  7.6 2.5 %reshape.306.hidden = bf16[64,7168]{1,0:T(8,128)(2,1)S(1)} reshape(bf16[32,2,7168]{2,1,0:T(2,128)(2,1)} %param.18) | data formatting | bytes 1835008 | tf_op jit(solution)/shard_map/reshape | solution.py:753
  10.2 12.5 %copy.37.w_dkv = bf16[7168,576]{1,0:T(8,128)(2,1)} copy(bf16[7168,576]{0,1:T(8,128)(2,1)} %param.14) | data formatting | bytes 16515072 | tf_op args[1]
  22.7 57.4 %shard_map.127 = (bf16[8,4,192,512]{3,2,1,0:T(8,128)(2,1)}, bf16[8,4,96,128]{3,2,1,0:T(8,128)(2,1)S(1)}, bf16[4,256,512]{2,1,0:T(8,128)(2,1)}, bf16[4,256,128]{2...) custom-call(s32[12]{0:T(128)S(1)} %select_reduce_fusion.4.send_idx, ...), custom_call_target="tpu_custom_call" | custom-call | tf_op jit(solution)/shard_map/pallas_call | solution.py:758
  80.1 1.2 copy-done
  81.4 17.7 %shard_map.128 = (bf16[4,256,512]{2,1,0:T(8,128)(2,1)S(1)}, f32[4,8,256]{2,1,0:T(8,128)S(1)}) custom-call(s32[96]{0:T(128)S(1)} %get-tuple-element.22.order, s32[96]{0:T(128)S(1)} %get-tuple-element.21.owner, s32[2]{0:T(128)S(1)} %pad_add_fusion.count, bf16[6144,512]{1,0:T(8,128)(2,1)} %bitcast.18, bf16[3072,128]{1,0:T(8,128)(2,1)S(1)} %bitcast.16, ...), custom_call_target="tpu_custom_call" | custom-call | tf_op jit(solution)/shard_map/pallas_call | solution.py:824
  99.1 39.0 %shard_map.129 = bf16[64,224]{1,0:T(8,128)(2,1)S(1)} custom-call(bf16[4,256,512]{2,1,0:T(8,128)(2,1)S(1)} %get-tuple-element.19.part, f32[4,8,256]{2,1,0:T(8,128)S(1)} %get-tuple-element.20.stats, bf16[4,512,128]{2,1,0:T(8,128)(2,1)S(1)} %copy-done.2, bf16[512,7168]{1,0:T(8,128)(2,1)} %w_o.1), custom_call_target="tpu_custom_call" | custom-call | tf_op jit(solution)/shard_map/pallas_call | solution.py:853
  138.1 0.6 reshape.314
  (34 shorter events, 1.3 us)
Async XLA Ops:
  10.1 12.5 %copy-start.1 = (bf16[224,1536]{1,0:T(8,128)(2,1)S(1)}, bf16[224,1536]{1,0:T(8,128)(2,1)}, u32[]{:S(2)}) copy-start(bf16[224,1536]{1,0:T(8,128)(2,1)} %w_dq.1) | copy-start | bytes 2064388
  10.1 12.5 %copy-start.3 = (bf16[4,128,512]{2,1,0:T(8,128)(2,1)S(1)}, bf16[4,128,512]{2,1,0:T(8,128)(2,1)}, u32[]{:S(2)}) copy-start(bf16[4,128,512]{2,1,0:T(8,128)(2,1)} %w_uk.1) | copy-start | bytes 1572868
  10.2 12.5 %copy-start.4 = (f32[512]{0:T(512)S(1)}, f32[512]{0:T(512)}, u32[]{:S(2)}) copy-start(f32[512]{0:T(512)} %param.15) | copy-start | bytes 6148
  80.1 1.2 copy-start
  81.3 17.8 %copy-start.2 = (bf16[4,512,128]{2,1,0:T(8,128)(2,1)S(1)}, bf16[4,512,128]{2,1,0:T(8,128)(2,1)}, u32[]{:S(2)}) copy-start(bf16[4,512,128]{2,1,0:T(8,128)(2,1)} %w_uv.1) | copy-start | bytes 1572868
where the time goes:
time: 139 us
  Pallas kernels  114 us (82%)
  local copies, waits for them, and re-layouts  18.9 us (14%)
  other arithmetic  5.52 us (4%)
    pallas_call x1, Pallas kernels, on_device(): pl.pallas_call(gather_kernel, out_shape=[jax.ShapeDtypeStruct((NB, NG, RO...  57.4 us
    pallas_call x1, Pallas kernels, on_device(): pl.pallas_call(project_kernel, out_shape=jax.ShapeDtypeStruct((64, width)...  39 us
    pallas_call x1, Pallas kernels, on_device(): pl.pallas_call(attend_kernel, out_shape=[jax.ShapeDtypeStruct((NY, 256, L...  17.7 us
    unnamed x11, local copies, waits for them, and re-layouts  13.7 us

commit v1 on v0

v1 whole, which is shorter than its diff:
```python
import jax
import jax.numpy as jnp
from jax import lax
from jax.experimental import pallas as pl
from jax.experimental.pallas import tpu as pltpu
from jax.sharding import PartitionSpec as P

PAGE = 64
SLOT = 3
MAXP = 16
LAT = 512
ROPE = 64
NOPE = 128
QL = 1536
NH = 4
NG = 4
NY = 4
NB = 8
N_HEAD = 32
ROWS = SLOT * PAGE
RROWS = SLOT * PAGE // 2
KCHUNK = 1024
OFFS = (0, 1, 3, 2)
MESH = pl.DeviceIdType.MESH
F32 = jnp.float32
BF16 = jnp.bfloat16
LOW = -1e30


def dot(a, b):
    return jnp.dot(a, b, preferred_element_type=F32)


def dot_t(a, b):
    return lax.dot_general(a, b, (((1,), (1,)), ((), ())), preferred_element_type=F32)


def norm_rows(values, gain_row, width):
    mean = jnp.sum(values * values, axis=-1, keepdims=True) * (1.0 / width)
    return values * lax.rsqrt(mean + 1e-06) * gain_row


def rotate_pairs(x, cosine, signed_sine):
    lane = lax.broadcasted_iota(jnp.int32, x.shape, 1)
    swapped = jnp.where((lane & 63) < 32, pltpu.roll(x, 96, 1), pltpu.roll(x, 32, 1))
    return x * cosine + swapped * signed_sine


def rows_by_request(transposed):
    i = lax.broadcasted_iota(jnp.int32, (256, 256), 1 if transposed else 0)
    j = lax.broadcasted_iota(jnp.int32, (256, 256), 0 if transposed else 1)
    place = ((i >> 1) & 3) * 64 + (i >> 3) * 2 + (i & 1)
    return jnp.where(j == place, 1.0, 0.0).astype(BF16)


def fused_kernel(
    send_idx,
    owner,
    listed,
    hpart,
    w_dq,
    kv_gain,
    q_gain,
    page_cos,
    page_sin,
    new_cos,
    new_sin,
    prompt,
    hidden,
    w_dkv,
    w_uq,
    w_uk,
    w_uv,
    w_o,
    out,
    pbuf,
    hbuf,
    wbuf,
    acc,
    uq_buf,
    uk_buf,
    uv_buf,
    lat_own,
    rope_own,
    zlat,
    zrope,
    qpart,
    rq_land,
    red,
    qlat,
    qmine,
    qrmine,
    new_lat,
    new_rope,
    new_o,
    new_lse,
    lat_all,
    rope_all,
    q_lat,
    q_rope,
    qf,
    qb,
    o_slot,
    m_slot,
    l_slot,
    part,
    lse_rows,
    stats,
    o_land,
    s_land,
    t_buf,
    vals,
    sbuf,
    sib_land,
    tbuf,
    rbuf,
    load_sem,
    w_sem,
    own_sem,
    z_send,
    z_recv,
    x_send,
    x_recv,
    f_send,
    f_recv,
    c_send,
    c_recv,
    r_send,
    r_recv,
    g_send,
    g_recv,
    y_send,
    y_recv,
    o_send,
    o_recv,
    p_send,
    p_recv,
    d_send,
    d_recv,
):
    g = lax.axis_index("grp")
    h = lax.axis_index("head")
    y = h // NB
    b = h % NB
    x = b // 2
    c = b % 2
    other = 1 - c
    sibling = y * NB + x * 2 + other
    right = y * NB + ((x + 1) % 4) * 2 + c
    left = y * NB + ((x + 3) % 4) * 2 + c
    scale = (NOPE + ROPE) ** (-0.5)

    def start(copies):
        for one in copies:
            one.start()

    def wait_recv(copies):
        for one in copies:
            one.wait_recv()

    def wait_send(copies):
        for one in copies:
            one.wait_send()

    def remote(src, dst, send, recv, to):
        return pltpu.make_async_remote_copy(
            src_ref=src,
            dst_ref=dst,
            send_sem=send,
            recv_sem=recv,
            device_id=to,
            device_id_type=MESH,
        )

    barrier = pltpu.get_barrier_semaphore()

    @pl.loop(1, N_HEAD)
    def _(o):
        pl.semaphore_signal(
            barrier, inc=1, device_id={"head": (h + o) % N_HEAD}, device_id_type=MESH
        )

    for o in (1, 2, 3):
        pl.semaphore_signal(barrier, inc=1, device_id={"grp": (g + o) % NG}, device_id_type=MESH)

    depth = prompt.shape[1]
    tokens = prompt.shape[0]
    chunks = depth // KCHUNK
    loads = []
    for k in range(chunks):
        cols = pl.ds(k * KCHUNK, KCHUNK)
        loads.append(
            [
                pltpu.make_async_copy(
                    prompt.at[:, cols], pbuf.at[pl.ds(0, tokens), cols], load_sem.at[k, 0]
                ),
                pltpu.make_async_copy(
                    hidden.at[:, :, cols], hbuf.at[:, :, cols], load_sem.at[k, 1]
                ),
                pltpu.make_async_copy(w_dkv.at[:, cols], wbuf.at[:, cols], load_sem.at[k, 2]),
            ]
        )
    for group in loads:
        start(group)
    uq_copy = pltpu.make_async_copy(w_uq, uq_buf, w_sem.at[0])
    uk_copy = pltpu.make_async_copy(w_uk, uk_buf, w_sem.at[1])
    uv_copy = pltpu.make_async_copy(w_uv, uv_buf, w_sem.at[2])
    wo_copy = pltpu.make_async_copy(w_o, wbuf.at[pl.ds(0, w_o.shape[0])], w_sem.at[3])
    start([uq_copy, uk_copy, uv_copy])

    qpart[...] = dot(hpart[...], w_dq[...])
    pl.semaphore_wait(barrier, N_HEAD - 1 + 3)

    def q_block(i):
        return (
            pl.ds(pl.multiple_of((i // 4) * 8, 8), 8),
            pl.ds(pl.multiple_of((i % 4) * 384, 128), 384),
        )

    def share_copy(to):
        return remote(qpart.at[q_block(to)], rq_land.at[h], r_send.at[to], r_recv.at[h], {"head": to})

    def sum_copy(to):
        return remote(red, qlat.at[q_block(h)], g_send.at[to], g_recv.at[h], {"head": to})

    @pl.loop(1, N_HEAD)
    def _(o):
        share_copy((h + o) % N_HEAD).start()

    for k in range(chunks):
        if k == 4:
            rq_land[h] = qpart[q_block(h)]

            @pl.loop(1, N_HEAD)
            def _(o):
                src = (h + o) % N_HEAD
                remote(
                    rq_land.at[src], rq_land.at[src], r_send.at[src], r_recv.at[src], {"head": src}
                ).wait_recv()

            red[...] = jnp.sum(rq_land[...], axis=0)
            qlat[q_block(h)] = red[...]

            @pl.loop(1, N_HEAD)
            def _(o):
                sum_copy((h + o) % N_HEAD).start()

        for one in loads[k]:
            one.wait()
        cols = slice(k * KCHUNK, (k + 1) * KCHUNK)
        pbuf[tokens:, cols] = hbuf[:, :, cols].reshape(64, KCHUNK)
        piece = dot_t(pbuf[:, cols], wbuf[:, cols])
        if k == 0:
            acc[...] = piece
        else:
            acc[...] += piece
    wo_copy.start()

    pages = tokens // PAGE
    lat_own[...] = (
        norm_rows(acc[0:tokens, 0:LAT], kv_gain[...], LAT).astype(BF16).reshape(pages, PAGE, LAT)
    )
    halves = []
    for p in range(pages):
        first = acc[p * PAGE : p * PAGE + 32, LAT : LAT + ROPE]
        second = acc[p * PAGE + 32 : p * PAGE + 64, LAT : LAT + ROPE]
        halves.append(jnp.concatenate([first, second], axis=1))
    packed = jnp.concatenate(halves, axis=0)
    rope_own[...] = (
        rotate_pairs(packed, page_cos[...], page_sin[...]).astype(BF16).reshape(pages, 32, 128)
    )

    for j in range(4):
        rank = (g + OFFS[j]) % NG
        for k in range(SLOT):
            page = send_idx[rank * SLOT + k]
            zlat[j, k * PAGE : (k + 1) * PAGE, :] = lat_own[page]
            zrope[j, k * 32 : (k + 1) * 32, :] = rope_own[page]

    def z_copies(j):
        rank = (g + OFFS[j]) % NG
        return [
            remote(
                src.at[j], dst.at[b, g], z_send.at[j - 1, i], z_recv.at[j - 1, i], {"grp": rank}
            )
            for i, (src, dst) in enumerate(((zlat, lat_all), (zrope, rope_all)))
        ]

    def plane(j):
        return (g + NG - OFFS[j]) % NG

    def block_at(dx, core):
        return ((x + dx) % 4) * 2 + core

    def ring_copies(j, dx, to, send, recv):
        gs = plane(j)
        at = block_at(dx, c)
        res = []
        for i, (mine, ref) in enumerate(((zlat, lat_all), (zrope, rope_all))):
            src = mine.at[0] if (j == 0 and dx == 0) else ref.at[at, gs]
            res.append(remote(src, ref.at[at, gs], send.at[i], recv.at[i], {"head": to}))
        return res

    def to_right(j):
        return ring_copies(j, 0, right, x_send.at[j, 0], x_recv.at[j, 0])

    def to_left(j):
        return ring_copies(j, 0, left, x_send.at[j, 1], x_recv.at[j, 1])

    def onward(j):
        if j in (0, 3):
            return ring_copies(j, 3, right, f_send.at[j], f_recv.at[j])
        return ring_copies(j, 1, left, f_send.at[j], f_recv.at[j])

    def across(j, dx):
        return ring_copies(j, dx, sibling, c_send.at[j, dx], c_recv.at[j, dx])

    def arrived(j, dx, core, sem):
        gs = plane(j)
        at = block_at(dx, core)
        for i, ref in enumerate((lat_all, rope_all)):
            remote(
                ref.at[at, gs], ref.at[at, gs], sem.at[i], sem.at[i], {"head": sibling}
            ).wait_recv()

    def serve_own(j):
        if j > 0:
            arrived(j, 0, c, z_recv.at[j - 1])
        start(to_right(j))
        start(to_left(j))
        start(across(j, 0))

    def serve_near(j):
        arrived(j, 3, c, x_recv.at[j, 0])
        if j in (0, 3):
            start(onward(j))
        start(across(j, 3))
        arrived(j, 1, c, x_recv.at[j, 1])
        if j in (1, 2):
            start(onward(j))
        start(across(j, 1))

    def serve_far(j):
        arrived(j, 2, c, f_recv.at[j])
        start(across(j, 2))

    def from_sibling(j, places):
        for dx in places:
            arrived(j, dx, other, c_recv.at[j, dx])

    for j in (1, 2, 3):
        start(z_copies(j))
    own = [
        pltpu.make_async_copy(zlat.at[0], lat_all.at[b, g], own_sem.at[0]),
        pltpu.make_async_copy(zrope.at[0], rope_all.at[b, g], own_sem.at[1]),
    ]
    start(own)
    serve_own(0)

    new_lat[...] = norm_rows(acc[tokens : tokens + 64, 0:LAT], kv_gain[...], LAT).astype(BF16)
    new_r = acc[tokens : tokens + 64, LAT : LAT + ROPE]
    new_r = rotate_pairs(jnp.concatenate([new_r, new_r], axis=1), new_cos[...], new_sin[...])
    lane = lax.broadcasted_iota(jnp.int32, new_r.shape, 1)
    new_rope[...] = jnp.where(lane < ROPE, new_r, 0.0).astype(BF16)

    @pl.loop(1, N_HEAD)
    def _(o):
        src = (h + o) % N_HEAD
        remote(
            red, qlat.at[q_block(src)], g_send.at[src], g_recv.at[src], {"head": src}
        ).wait_recv()

    uq_copy.wait()
    uk_copy.wait()
    query_norm = norm_rows(qlat[...], q_gain[...], QL).astype(BF16)
    queries = dot(query_norm, uq_buf[...])
    parts = []
    ropes = []
    for n in range(NH):
        at = n * (NOPE + ROPE)
        parts.append(dot(queries[:, at : at + NOPE].astype(BF16), uk_buf[n]).astype(BF16))
        one = queries[:, at + NOPE : at + NOPE + ROPE]
        one = jnp.concatenate([one, one], axis=1)
        ropes.append(rotate_pairs(one, new_cos[...], new_sin[...]).astype(BF16))
    order = rows_by_request(False)
    qmine[...] = dot(order, jnp.concatenate(parts, axis=0)).astype(BF16)
    qrmine[...] = dot(order, jnp.concatenate(ropes, axis=0)).astype(BF16)

    def y_copies(o):
        to = ((y + o) % NY) * NB + b
        return [
            remote(src, dst.at[y], y_send.at[o - 1, i], y_recv.at[o - 1, i], {"head": to})
            for i, (src, dst) in enumerate(((qmine, q_lat), (qrmine, q_rope)))
        ]

    for o in (2, 1, 3):
        start(y_copies(o))
    q_lat[y] = qmine[...]
    q_rope[y] = qrmine[...]

    serve_near(0)
    serve_own(1)
    serve_own(2)
    serve_far(0)
    serve_own(3)

    s = (dot_t(qmine[...], new_lat[...]) + dot_t(qrmine[...], new_rope[...])) * scale
    i = lax.broadcasted_iota(jnp.int32, s.shape, 0)
    j = lax.broadcasted_iota(jnp.int32, s.shape, 1)
    live = ((i >> 3) == (j >> 1)) & ((j & 1) <= (i & 1))
    s = jnp.where(live, s, LOW)
    top = jnp.max(s, axis=1, keepdims=True)
    p = jnp.where(live, jnp.exp(s - top), 0.0)
    total = jnp.sum(p, axis=1, keepdims=True)
    new_o[...] = dot(p.astype(BF16), new_lat[...]) / total
    new_lse[...] = jnp.broadcast_to(top + jnp.log(total), new_lse.shape)

    serve_near(1)

    for o in (1, 3, 2):
        src = (y + NY - o) % NY
        for n, ref in enumerate((q_lat, q_rope)):
            remote(
                ref.at[src],
                ref.at[src],
                y_send.at[o - 1, n],
                y_recv.at[o - 1, n],
                {"head": src * NB + b},
            ).wait_recv()
    requests = 32
    for yb in range(NY):
        qf[:, yb * 8 : (yb + 1) * 8, 0:LAT] = q_lat[yb].astype(F32).reshape(requests, 8, LAT)
        qf[:, yb * 8 : (yb + 1) * 8, LAT:] = q_rope[yb].astype(F32).reshape(requests, 8, 128)
    qb[0:requests] = qf[...].astype(BF16)
    qb[requests] = jnp.zeros((32, LAT + 128), BF16)

    row = lax.broadcasted_iota(jnp.int32, (SLOT * 32, ROWS), 0)
    col = lax.broadcasted_iota(jnp.int32, (SLOT * 32, ROWS), 1)
    own_page = (row >> 5) == (col >> 6)
    low_lane = lax.broadcasted_iota(jnp.int32, (32, 128), 1) < ROPE

    def attend(at, gs):
        first = (at * NG + gs) * SLOT
        keys = lat_all[at, gs]
        pairs = rope_all[at, gs]
        zero = jnp.zeros((32, 128), BF16)
        ropes = []
        for k in range(SLOT):
            pair = pairs[k * 32 : (k + 1) * 32, :]
            ropes += [jnp.where(low_lane, pair, zero), jnp.where(low_lane, zero, pair)]
        q = jnp.concatenate([qb[owner[first + k]] for k in range(SLOT)], axis=0)
        s = dot_t(q[:, 0:LAT], keys) + dot_t(q[:, LAT:], jnp.concatenate(ropes, axis=0))
        s = jnp.where(own_page, s * scale, LOW)
        top = jnp.max(s, axis=1, keepdims=True)
        p = jnp.where(own_page, jnp.exp(s - top), 0.0)
        total = jnp.sum(p, axis=1, keepdims=True)
        o = dot(p.astype(BF16), keys)
        top = jnp.broadcast_to(top, (SLOT * 32, 128))
        total = jnp.broadcast_to(total, (SLOT * 32, 128))
        o_slot[pl.ds(first, SLOT)] = o.astype(BF16).reshape(SLOT, 32, LAT)
        m_slot[pl.ds(first, SLOT)] = top.reshape(SLOT, 32, 128)
        l_slot[pl.ds(first, SLOT)] = total.reshape(SLOT, 32, 128)

    def gray(j):
        return j ^ (j >> 1)

    def attend_own(n, core, dx, j0):
        @pl.loop(0, n // 2)
        def _(i):
            for u in range(2):
                attend(block_at(dx, core), (g + NG - gray(j0 + 2 * i + u)) % NG)

    def attend_places(j, core, places):
        for dx in places:
            attend(block_at(dx, core), plane(j))

    def attend_ring(j, core):
        @pl.loop(0, 2)
        def _(i):
            for u in range(2):
                attend(block_at(2 * i + u, core), plane(j))

    for one in own:
        one.wait()
    o_slot[96] = jnp.zeros((32, LAT), BF16)
    m_slot[96] = jnp.full((32, 128), LOW, F32)
    l_slot[96] = jnp.zeros((32, 128), F32)
    attend_own(4, c, 0, 0)
    serve_near(2)
    attend_places(0, c, (1, 3))
    serve_far(1)
    attend_places(0, c, (2,))
    attend_places(1, c, (1, 3))
    serve_far(2)
    from_sibling(0, (0, 1, 2, 3))
    attend_ring(0, other)
    serve_near(3)
    attend_places(2, c, (1, 3))
    attend_places(1, c, (2,))
    from_sibling(1, (0, 1, 2, 3))
    attend_ring(1, other)
    serve_far(3)
    attend_places(2, c, (2,))
    attend_places(3, c, (1, 3))
    from_sibling(2, (0, 1, 2, 3))
    attend_ring(2, other)
    attend_places(3, c, (2,))
    from_sibling(3, (0, 1, 2, 3))
    attend_ring(3, other)

    @pl.loop(0, requests // 2)
    def _(pair):
        mixes = []
        for u in range(2):
            r = pair * 2 + u
            at = [listed[r * MAXP + k] for k in range(MAXP)]
            tops = [m_slot[one] for one in at]
            top = tops[0]
            for one in tops[1:]:
                top = jnp.maximum(top, one)
            total = jnp.zeros((32, 128), F32)
            mixed = jnp.zeros((32, LAT), F32)
            for one, its_top in zip(at, tops):
                e = jnp.exp(its_top - top)
                total += l_slot[one] * e
                mixed += o_slot[one].astype(F32) * e[:, 0:1]
            some = total > 0.0
            safe = jnp.where(some, total, 1.0)
            lse = jnp.where(some, top + jnp.log(safe), LOW)
            mixed = mixed * (1.0 / safe)[:, 0:1]
            mixes.append(mixed)
            for yb in range(NY):
                lse_rows[yb, pl.ds(pl.multiple_of(r * 8, 8), 8), :] = lse[yb * 8 : (yb + 1) * 8]
        for yb in range(NY):
            rows = slice(yb * 8, (yb + 1) * 8)
            both = jnp.concatenate([mixes[0][rows], mixes[1][rows]], axis=0)
            part[yb, pl.ds(pl.multiple_of(pair * 16, 16), 16), :] = both.astype(BF16)

    for yb in range(NY):
        stats[yb] = jnp.transpose(lse_rows[yb])[0:8, :]

    def o_copies(o):
        ty = (y + o) % NY
        return [
            remote(
                src.at[ty],
                dst.at[o - 1],
                o_send.at[o - 1, i],
                o_recv.at[o - 1, i],
                {"head": ty * NB + b},
            )
            for i, (src, dst) in enumerate(((part, o_land), (stats, s_land)))
        ]

    for o in (2, 1, 3):
        start(o_copies(o))

    def column(block):
        t_buf[0:8, :] = block
        return jnp.transpose(t_buf[...])[:, 0:1]

    t_buf[...] = jnp.zeros_like(t_buf)
    lses = [new_lse[:, 0:1], column(stats[y])]
    mixes = [new_o[...], part[y].astype(F32)]
    for o in (1, 3, 2):
        wait_recv(o_copies(o))
        lses.append(column(s_land[o - 1]))
        mixes.append(o_land[o - 1].astype(F32))
    top = lses[0]
    for one in lses[1:]:
        top = jnp.maximum(top, one)
    weights = [jnp.exp(one - top) for one in lses]
    total = weights[0]
    for one in weights[1:]:
        total = total + one
    mixed = mixes[0] * (weights[0] / total)
    for one, weight in zip(mixes[1:], weights[1:]):
        mixed += one * (weight / total)
    by_head = dot(rows_by_request(True), mixed.astype(BF16)).astype(BF16)
    uv_copy.wait()
    for n in range(NH):
        vals[:, n * 128 : (n + 1) * 128] = dot(
            by_head[n * 64 : (n + 1) * 64, :], uv_buf[n]
        ).astype(BF16)

    wo_copy.wait()
    width = out.shape[1]
    span = width * NB
    chip = y * 4 + x

    def pair_copy(ty):
        chips = pl.ds(ty * 4, 4)
        return remote(
            sbuf.at[other, chips], sib_land.at[chips], p_send.at[ty], p_recv.at[ty], {"head": sibling}
        )

    for n in range(NY):
        ty = (y + n) % NY
        cols = pl.ds(pl.multiple_of(ty * span, 128), span)
        piece = dot(vals[...], wbuf[0 : w_o.shape[0], cols])
        for k in range(NB):
            sbuf[k % 2, ty * 4 + k // 2] = piece[:, k * width : (k + 1) * width].astype(BF16)
        pair_copy(ty).start()

    def out_copy(t):
        return remote(
            tbuf.at[t], rbuf.at[chip], d_send.at[t], d_recv.at[chip], {"head": t * 2 + c}
        )

    for n in (1, 2, 3, 0):
        ty = (y + n) % NY
        pair_copy(ty).wait_recv()
        for k in range(4):
            t = ty * 4 + k
            tbuf[t] = (sbuf[c, t].astype(F32) + sib_land[t].astype(F32)).astype(BF16)

            @pl.when(t != chip)
            def _():
                out_copy(t).start()

    def body(o, total):
        src = (chip + o) % 16
        remote(
            rbuf.at[src], rbuf.at[src], d_send.at[src], d_recv.at[src], {"head": src * 2 + c}
        ).wait_recv()
        return total + rbuf[src].astype(F32)

    result = lax.fori_loop(1, 16, body, tbuf[chip].astype(F32))
    out[...] = result.astype(BF16)

    for j in (1, 2, 3):
        wait_send(z_copies(j))
    for j in range(4):
        wait_send(to_right(j))
        wait_send(to_left(j))
        wait_send(onward(j))
        for dx in range(4):
            wait_send(across(j, dx))
    for o in (1, 2, 3):
        wait_send(y_copies(o))
        wait_send(o_copies(o))
    for ty in range(NY):
        pair_copy(ty).wait_send()

    @pl.loop(1, 16)
    def _(o):
        out_copy((chip + o) % 16).wait_send()

    @pl.loop(1, N_HEAD)
    def _(o):
        to = (h + o) % N_HEAD
        share_copy(to).wait_send()
        sum_copy(to).wait_send()


def spec(space):
    return pl.BlockSpec(memory_space=space)


VM, SM, ANY = pltpu.VMEM, pltpu.SMEM, pl.ANY


def page_plan(block_table, ctx_pages, g, y, b, per_rank, pages_dev):
    flat = jnp.where(
        jnp.arange(MAXP, dtype=jnp.int32)[None, :] < ctx_pages[:, None], block_table, -1
    ).reshape(1, -1)
    at = jnp.arange(NG * NB * pages_dev, dtype=jnp.int32)
    per_plane = NB * pages_dev
    ids = (at // per_plane) * (N_HEAD * pages_dev) + y * per_plane + at % per_plane
    codes = jnp.arange(flat.shape[1], dtype=jnp.int32)[None, :]
    code = jnp.sum(jnp.where(flat == ids[:, None], codes, 0), axis=1)
    code = code.reshape(NG, NB, pages_dev)
    target = code // (per_rank * MAXP)
    within = jnp.arange(pages_dev, dtype=jnp.int32)
    alike = (target[..., :, None] == target[..., None, :]) & (within[None, :] < within[:, None])
    slot = jnp.sum(alike.astype(jnp.int32), axis=-1)
    places = jnp.arange(SLOT, dtype=jnp.int32)
    here = (target == g)[..., None, :] & (slot[..., None, :] == places[:, None])
    local = code % (per_rank * MAXP)
    held = jnp.sum(jnp.where(here, local[..., None, :] + 1, 0), axis=-1) - 1
    held = held.transpose(1, 0, 2).reshape(-1)
    owner = jnp.where(held >= 0, held // MAXP, per_rank)
    wanted = jnp.arange(per_rank * MAXP, dtype=jnp.int32)
    total = held.shape[0]
    spare = jnp.arange(total, dtype=jnp.int32) - total
    listed = total + jnp.sum(jnp.where(held[None, :] == wanted[:, None], spare[None, :], 0), axis=1)
    mine = lax.dynamic_slice(code, (g, b, 0), (1, 1, pages_dev)).reshape(-1)
    my_target = lax.dynamic_slice(target, (g, b, 0), (1, 1, pages_dev)).reshape(-1)
    my_slot = lax.dynamic_slice(slot, (g, b, 0), (1, 1, pages_dev)).reshape(-1)
    sends = (my_target[None, :] * SLOT + my_slot[None, :]) == jnp.arange(
        NG * SLOT, dtype=jnp.int32
    )[:, None]
    send_idx = jnp.sum(jnp.where(sends, within[None, :], 0), axis=1)
    return owner, listed, send_idx, mine % MAXP


def angle_tables(positions):
    lane = jnp.arange(2 * ROPE, dtype=jnp.int32)
    inverse_freq = 10000.0 ** (-2.0 * (lane % 32).astype(F32) / ROPE)
    angles = jnp.repeat(positions.astype(F32), ROPE, axis=1) * inverse_freq[None, :]
    sign = jnp.where((lane % ROPE) < 32, -1.0, 1.0).astype(F32)
    return jnp.cos(angles), jnp.sin(angles) * sign[None, :]


def on_device(
    prompt, w_dkv, kv_gain, block_table, ctx_pages, dec_hidden, w_dq, q_gain, w_uq, w_uk, w_uv, w_o
):
    g = lax.axis_index("grp")
    h = lax.axis_index("head")
    y, b = h // NB, h % NB
    tokens, depth = prompt.shape
    pages_dev = tokens // PAGE
    per_rank = dec_hidden.shape[0]
    owner, listed, send_idx, my_depth = page_plan(
        block_table, ctx_pages, g, y, b, per_rank, pages_dev
    )
    lengths = lax.dynamic_slice_in_dim(ctx_pages, g * per_rank, per_rank, 0)
    t = jnp.arange(32, dtype=jnp.int32)
    page_pos = my_depth[:, None, None] * PAGE + t[None, :, None] + jnp.array([0, 32], jnp.int32)
    page_cos, page_sin = angle_tables(page_pos.reshape(-1, 2))
    new_pos = (lengths[:, None] * PAGE + jnp.arange(2, dtype=jnp.int32)[None, :]).reshape(-1, 1)
    new_cos, new_sin = angle_tables(jnp.concatenate([new_pos, new_pos], axis=1))
    share = w_dq.shape[0]
    hpart = lax.dynamic_slice_in_dim(dec_hidden, h * share, share, 2).reshape(-1, share)

    dma = pltpu.SemaphoreType.DMA
    width = depth // N_HEAD
    slots = NB * NG * SLOT
    out = pl.pallas_call(
        fused_kernel,
        out_shape=jax.ShapeDtypeStruct((64, width), BF16),
        in_specs=[spec(SM)] * 3 + [spec(VM)] * 8 + [spec(ANY)] * 7,
        out_specs=spec(VM),
        scratch_shapes=[
            pltpu.VMEM((tokens + 64, depth), BF16),
            pltpu.VMEM((per_rank, 2, depth), BF16),
            pltpu.VMEM((LAT + ROPE, depth), BF16),
            pltpu.VMEM((tokens + 64, LAT + ROPE), F32),
            pltpu.VMEM(w_uq.shape, BF16),
            pltpu.VMEM(w_uk.shape, BF16),
            pltpu.VMEM(w_uv.shape, BF16),
            pltpu.VMEM((pages_dev, PAGE, LAT), BF16),
            pltpu.VMEM((pages_dev, 32, 128), BF16),
            pltpu.VMEM((NG, ROWS, LAT), BF16),
            pltpu.VMEM((NG, RROWS, 128), BF16),
            pltpu.VMEM((64, QL), F32),
            pltpu.VMEM((N_HEAD, 8, 384), F32),
            pltpu.VMEM((8, 384), F32),
            pltpu.VMEM((64, QL), F32),
            pltpu.VMEM((256, LAT), BF16),
            pltpu.VMEM((256, 128), BF16),
            pltpu.VMEM((64, LAT), BF16),
            pltpu.VMEM((64, 128), BF16),
            pltpu.VMEM((256, LAT), F32),
            pltpu.VMEM((256, 128), F32),
            pltpu.VMEM((NB, NG, ROWS, LAT), BF16),
            pltpu.VMEM((NB, NG, RROWS, 128), BF16),
            pltpu.VMEM((NY, 256, LAT), BF16),
            pltpu.VMEM((NY, 256, 128), BF16),
            pltpu.VMEM((32, 32, LAT + 128), F32),
            pltpu.VMEM((33, 32, LAT + 128), BF16),
            pltpu.VMEM((slots + 1, 32, LAT), BF16),
            pltpu.VMEM((slots + 1, 32, 128), F32),
            pltpu.VMEM((slots + 1, 32, 128), F32),
            pltpu.VMEM((NY, 256, LAT), BF16),
            pltpu.VMEM((NY, 256, 128), F32),
            pltpu.VMEM((NY, 8, 256), F32),
            pltpu.VMEM((3, 256, LAT), BF16),
            pltpu.VMEM((3, 8, 256), F32),
            pltpu.VMEM((128, 256), F32),
            pltpu.VMEM((64, LAT), BF16),
            pltpu.VMEM((2, 16, 64, width), BF16),
            pltpu.VMEM((16, 64, width), BF16),
            pltpu.VMEM((16, 64, width), BF16),
            pltpu.VMEM((16, 64, width), BF16),
            dma((depth // KCHUNK, 3)),
            dma((4,)),
            dma((2,)),
            dma((3, 2)),
            dma((3, 2)),
            dma((4, 2, 2)),
            dma((4, 2, 2)),
            dma((4, 2)),
            dma((4, 2)),
            dma((4, 4, 2)),
            dma((4, 4, 2)),
            dma((N_HEAD,)),
            dma((N_HEAD,)),
            dma((N_HEAD,)),
            dma((N_HEAD,)),
            dma((3, 2)),
            dma((3, 2)),
            dma((3, 2)),
            dma((3, 2)),
            dma((4,)),
            dma((4,)),
            dma((16,)),
            dma((16,)),
        ],
        compiler_params=pltpu.CompilerParams(
            collective_id=0, has_side_effects=True, vmem_limit_bytes=58 * 1024 * 1024
        ),
    )(
        send_idx,
        owner,
        listed,
        hpart,
        w_dq,
        kv_gain.reshape(1, -1),
        q_gain.reshape(1, -1),
        page_cos,
        page_sin,
        new_cos,
        new_sin,
        prompt,
        dec_hidden,
        w_dkv.T,
        w_uq,
        w_uk,
        w_uv,
        w_o,
    )
    return out.reshape(per_rank, 2, width)


def solution(mesh):
    return jax.shard_map(
        on_device,
        mesh=mesh,
        in_specs=(
            P(("grp", "head"), None),
            P(),
            P(),
            P(),
            P(),
            P("grp", None, None),
            P("head", None),
            P(),
            P(None, "head"),
            P("head", None, None),
            P("head", None, None),
            P("head", None),
        ),
        out_specs=P("grp", None, "head"),
        check_vma=False,
    )
```

time: 139 us -> 112 us (0.81)
  local copies, waits for them, and re-layouts: 18.9 us -> 4.77 us
  Pallas kernels: 114 us -> 101 us
    unnamed x11 -> x2, local copies, waits for them, and re-layouts: 13.7 us -> 0.01 us
    pallas_call x3 -> x1, Pallas kernels: 114 us -> 101 us  [on_device(): pl.pallas_call(fused_kernel, out_shape=jax.ShapeDtypeStruct((64, width),...]
    reshape x2, local copies, waits for them, and re-layouts: 2.59 us -> 0.76 us  [the longest x1 0.65 us: on_device(): lax.dynamic_slice_in_dim(dec_hidden, h * share, share, 2).reshape(-1, share)]
where the time goes in v1:
time: 112 us
  Pallas kernels  101 us (90%)
  other arithmetic  6.24 us (6%)
  local copies, waits for them, and re-layouts  4.77 us (4%)
    pallas_call x1, Pallas kernels, on_device(): pl.pallas_call(fused_kernel, out_shape=jax.ShapeDtypeStruct((64, width),...  101 us

profile of v1, /device:TPU:1, one launch (start us, length us, event | category | flops | bytes accessed | tf_op | source)
XLA Modules:
  0.0 111.7 jit_solution(5505798991596649628)
XLA Ops:
  0.0 0.7 fusion.3
  0.7 0.1 copy.26
  0.9 0.3 select_reduce_fusion
  1.3 0.1 reshape.271
  1.7 1.0 sine_multiply_fusion
  2.8 0.1 copy.27
  2.9 0.1 convert_reduce_fusion
  3.1 0.1 copy.31
  3.2 0.1 reshape.272
  3.3 0.1 select_reduce_fusion.1
  3.4 0.6 broadcast_add_fusion.listed
  4.0 0.5 compare_select_fusion.3.owner
  4.6 0.3 add_reduce_fusion
  4.8 0.7 select_reduce_fusion.3.send_idx
  5.5 0.7 dynamic-slice_multiply_fusion
  6.3 0.1 add.232
  6.5 0.1 broadcast_in_dim.110
  6.7 0.1 reshape.278
  6.8 0.8 sine_multiply_fusion.1
  7.5 0.9 constant_dynamic-slice_fusion.1
  8.5 0.7 reshape.273.hpart
  9.1 0.6 reshape.275.q_gain
  9.7 100.6 %shard_map.127 = bf16[64,224]{1,0:T(8,128)(2,1)} custom-call(s32[12]{0:T(128)} %select_reduce_fusion.3.send_idx, s32[96]{0:T(128)} %compare_select_fusion.3.owner, s32[512]{0:T(512)} %broadcast_add_fusion.listed, bf16[64,224]{1,0:T(8,128)(2,1)} %reshape.273.hpart, bf16[224,1536]{1,0:T(8,128)(2,1)} %w_dq.1, f32[1,512]{1,0:T(1,128)} %bitcast.13, ...), custom_call_target="tpu_custom_call" | custom-call | tf_op jit(solution)/shard_map/pallas_call | solution.py:729
  110.3 1.4 %reshape.279 = bf16[32,2,224]{2,1,0:T(2,128)(2,1)} reshape(bf16[64,224]{1,0:T(8,128)(2,1)} %shard_map.127) | data formatting | bytes 57344 | tf_op jit(solution)/shard_map/reshape | solution.py:823
  (21 shorter events, 0.7 us)
Async XLA Ops:
  0.0 9.1 %copy-start = (f32[1536]{0:T(1024)S(1)}, f32[1536]{0:T(1024)}, u32[]{:S(2)}) copy-start(f32[1536]{0:T(1024)} %param.20) | copy-start | bytes 18436

commit v2 on v1

--- a/solution.py
+++ b/solution.py
@@ -1,5 +1,6 @@
 import jax
 import jax.numpy as jnp
+import numpy as np
 from jax import lax
 from jax.experimental import pallas as pl
 from jax.experimental.pallas import tpu as pltpu
@@ -20,6 +21,7 @@
 ROWS = SLOT * PAGE
 RROWS = SLOT * PAGE // 2
 KCHUNK = 1024
+AHEAD = 3
 OFFS = (0, 1, 3, 2)
 MESH = pl.DeviceIdType.MESH
 F32 = jnp.float32
@@ -57,16 +59,17 @@
     send_idx,
     owner,
     listed,
-    hpart,
-    w_dq,
+    depths,
+    lengths,
     kv_gain,
     q_gain,
-    page_cos,
-    page_sin,
-    new_cos,
-    new_sin,
+    cos_far,
+    sin_far,
+    cos_near,
+    sin_near,
     prompt,
     hidden,
+    w_dq,
     w_dkv,
     w_uq,
     w_uk,
@@ -84,11 +87,17 @@
     rope_own,
     zlat,
     zrope,
+    wdq_buf,
+    new_cos,
+    new_sin,
     qpart,
+    pair_land,
+    half,
     rq_land,
     red,
     qlat,
     qmine,
+    qr_dup,
     qrmine,
     new_lat,
     new_rope,
@@ -125,6 +134,7 @@
     f_recv,
     c_send,
     c_recv,
+    q_sem,
     r_send,
     r_recv,
     g_send,
@@ -133,6 +143,8 @@
     y_recv,
     o_send,
     o_recv,
+    s_send,
+    s_recv,
     p_send,
     p_recv,
     d_send,
@@ -194,59 +206,121 @@
                 pltpu.make_async_copy(
                     prompt.at[:, cols], pbuf.at[pl.ds(0, tokens), cols], load_sem.at[k, 0]
                 ),
-                pltpu.make_async_copy(
-                    hidden.at[:, :, cols], hbuf.at[:, :, cols], load_sem.at[k, 1]
-                ),
-                pltpu.make_async_copy(w_dkv.at[:, cols], wbuf.at[:, cols], load_sem.at[k, 2]),
+                pltpu.make_async_copy(w_dkv.at[:, cols], wbuf.at[:, cols], load_sem.at[k, 1]),
             ]
         )
-    for group in loads:
+    share = w_dq.shape[0]
+    window = 384
+    first_col = jnp.minimum((h * share) // 128 * 128, depth - window)
+    at_row = pl.multiple_of(h * share - first_col, 32)
+    hidden_copy = pltpu.make_async_copy(hidden, hbuf, w_sem.at[4])
+    hidden_copy.start()
+    wdq_buf[...] = jnp.zeros_like(wdq_buf)
+    dq_copy = pltpu.make_async_copy(w_dq, wdq_buf.at[pl.ds(at_row, share), :], w_sem.at[5])
+    dq_copy.start()
+    for group in loads[:AHEAD]:
         start(group)
     uq_copy = pltpu.make_async_copy(w_uq, uq_buf, w_sem.at[0])
     uk_copy = pltpu.make_async_copy(w_uk, uk_buf, w_sem.at[1])
     uv_copy = pltpu.make_async_copy(w_uv, uv_buf, w_sem.at[2])
     wo_copy = pltpu.make_async_copy(w_o, wbuf.at[pl.ds(0, w_o.shape[0])], w_sem.at[3])
-    start([uq_copy, uk_copy, uv_copy])
-
-    qpart[...] = dot(hpart[...], w_dq[...])
-    pl.semaphore_wait(barrier, N_HEAD - 1 + 3)
-
-    def q_block(i):
+
+    requests = hidden.shape[0]
+    for r in range(requests):
+        far = lengths[g * requests + r]
+        new_cos[2 * r : 2 * r + 2, :] = jnp.broadcast_to(cos_far[pl.ds(far, 1), :], (2, 128))
+        new_sin[2 * r : 2 * r + 2, :] = jnp.broadcast_to(sin_far[pl.ds(far, 1), :], (2, 128))
+    odd = (lax.broadcasted_iota(jnp.int32, (64, 128), 0) & 1) == 1
+    step_cos = jnp.where(odd, cos_far[18:19, :], cos_far[17:18, :])
+    step_sin = jnp.where(odd, sin_far[18:19, :], sin_far[17:18, :])
+    far_cos, far_sin = new_cos[...], new_sin[...]
+    sign = jnp.where(
+        (lax.broadcasted_iota(jnp.int32, (1, 128), 1) & 63) < 32, -1.0, 1.0
+    ).astype(F32)
+    new_cos[...] = far_cos * step_cos - far_sin * step_sin
+    new_sin[...] = (far_sin * step_cos + far_cos * step_sin) * sign
+
+    hidden_copy.wait()
+    dq_copy.wait()
+    part_of_hidden = hbuf[:, :, pl.ds(pl.multiple_of(first_col, 128), window)].reshape(64, window)
+    qpart[...] = dot(part_of_hidden, wdq_buf[...])
+
+    chip = y * 4 + x
+    half_width = QL // 2
+
+    def half_cols(core):
+        return pl.ds(pl.multiple_of(core * half_width, 128), half_width)
+
+    def block_in(t, first):
         return (
-            pl.ds(pl.multiple_of((i // 4) * 8, 8), 8),
-            pl.ds(pl.multiple_of((i % 4) * 384, 128), 384),
-        )
-
-    def share_copy(to):
-        return remote(qpart.at[q_block(to)], rq_land.at[h], r_send.at[to], r_recv.at[h], {"head": to})
-
-    def sum_copy(to):
-        return remote(red, qlat.at[q_block(h)], g_send.at[to], g_recv.at[h], {"head": to})
-
-    @pl.loop(1, N_HEAD)
-    def _(o):
-        share_copy((h + o) % N_HEAD).start()
+            pl.ds(pl.multiple_of((t // 2) * 8, 8), 8),
+            pl.ds(pl.multiple_of(first + (t % 2) * 384, 128), 384),
+        )
+
+    def halves_copy():
+        return remote(
+            qpart.at[:, half_cols(other)], pair_land, q_sem.at[0], q_sem.at[1], {"head": sibling}
+        )
+
+    def share_copy(t):
+        return remote(
+            half.at[block_in(t, 0)], rq_land.at[chip], r_send.at[t], r_recv.at[chip], {"head": t * 2 + c}
+        )
+
+    def sum_copy(t):
+        return remote(
+            red,
+            qlat.at[block_in(chip, c * half_width)],
+            g_send.at[t],
+            g_recv.at[chip],
+            {"head": t * 2 + c},
+        )
+
+    def back_copy():
+        return remote(
+            qlat.at[:, half_cols(c)],
+            qlat.at[:, half_cols(c)],
+            q_sem.at[2],
+            q_sem.at[3],
+            {"head": sibling},
+        )
+
+    def share_sums():
+        halves_copy().wait_recv()
+        half[...] = qpart[:, half_cols(c)] + pair_land[...]
+        rq_land[chip] = half[block_in(chip, 0)]
+
+        @pl.loop(1, 16)
+        def _(o):
+            share_copy((chip + o) % 16).start()
+
+    def send_sums():
+        @pl.loop(1, 16)
+        def _(o):
+            src = (chip + o) % 16
+            remote(
+                rq_land.at[src], rq_land.at[src], r_send.at[src], r_recv.at[src], {"head": src * 2 + c}
+            ).wait_recv()
+
+        red[...] = jnp.sum(rq_land[...], axis=0)
+        qlat[block_in(chip, c * half_width)] = red[...]
+
+        @pl.loop(1, 16)
+        def _(o):
+            sum_copy((chip + o) % 16).start()
 
     for k in range(chunks):
-        if k == 4:
-            rq_land[h] = qpart[q_block(h)]
-
-            @pl.loop(1, N_HEAD)
-            def _(o):
-                src = (h + o) % N_HEAD
-                remote(
-                    rq_land.at[src], rq_land.at[src], r_send.at[src], r_recv.at[src], {"head": src}
-                ).wait_recv()
-
-            red[...] = jnp.sum(rq_land[...], axis=0)
-            qlat[q_block(h)] = red[...]
-
-            @pl.loop(1, N_HEAD)
-            def _(o):
-                sum_copy((h + o) % N_HEAD).start()
-
+        if k == 2:
+            pl.semaphore_wait(barrier, N_HEAD - 1 + 3)
+            halves_copy().start()
+        if k == 3:
+            share_sums()
         for one in loads[k]:
             one.wait()
+        if k + AHEAD < chunks:
+            start(loads[k + AHEAD])
+        elif k + AHEAD == chunks:
+            start([uq_copy, uk_copy, uv_copy])
         cols = slice(k * KCHUNK, (k + 1) * KCHUNK)
         pbuf[tokens:, cols] = hbuf[:, :, cols].reshape(64, KCHUNK)
         piece = dot_t(pbuf[:, cols], wbuf[:, cols])
@@ -254,11 +328,12 @@
             acc[...] = piece
         else:
             acc[...] += piece
+    send_sums()
     wo_copy.start()
 
     pages = tokens // PAGE
     lat_own[...] = (
-        norm_rows(acc[0:tokens, 0:LAT], kv_gain[...], LAT).astype(BF16).reshape(pages, PAGE, LAT)
+        norm_rows(acc[0:tokens, 0:LAT], kv_gain[...].reshape(1, LAT), LAT).astype(BF16).reshape(pages, PAGE, LAT)
     )
     halves = []
     for p in range(pages):
@@ -266,8 +341,17 @@
         second = acc[p * PAGE + 32 : p * PAGE + 64, LAT : LAT + ROPE]
         halves.append(jnp.concatenate([first, second], axis=1))
     packed = jnp.concatenate(halves, axis=0)
+    page_cos = []
+    page_sin = []
+    for p in range(pages):
+        far = pl.ds(depths[p], 1)
+        far_cos, far_sin = cos_far[far, :], sin_far[far, :]
+        page_cos.append(far_cos * cos_near[...] - far_sin * sin_near[...])
+        page_sin.append((far_sin * cos_near[...] + far_cos * sin_near[...]) * sign)
+    page_cos = jnp.concatenate(page_cos, axis=0)
+    page_sin = jnp.concatenate(page_sin, axis=0)
     rope_own[...] = (
-        rotate_pairs(packed, page_cos[...], page_sin[...]).astype(BF16).reshape(pages, 32, 128)
+        rotate_pairs(packed, page_cos, page_sin).astype(BF16).reshape(pages, 32, 128)
     )
 
     for j in range(4):
@@ -357,23 +441,37 @@
     start(own)
     serve_own(0)
 
-    new_lat[...] = norm_rows(acc[tokens : tokens + 64, 0:LAT], kv_gain[...], LAT).astype(BF16)
+    new_lat[...] = norm_rows(acc[tokens : tokens + 64, 0:LAT], kv_gain[...].reshape(1, LAT), LAT).astype(BF16)
     new_r = acc[tokens : tokens + 64, LAT : LAT + ROPE]
     new_r = rotate_pairs(jnp.concatenate([new_r, new_r], axis=1), new_cos[...], new_sin[...])
     lane = lax.broadcasted_iota(jnp.int32, new_r.shape, 1)
     new_rope[...] = jnp.where(lane < ROPE, new_r, 0.0).astype(BF16)
 
-    @pl.loop(1, N_HEAD)
+    @pl.loop(1, 16)
     def _(o):
-        src = (h + o) % N_HEAD
+        src = (chip + o) % 16
         remote(
-            red, qlat.at[q_block(src)], g_send.at[src], g_recv.at[src], {"head": src}
+            red,
+            qlat.at[block_in(src, c * half_width)],
+            g_send.at[src],
+            g_recv.at[src],
+            {"head": src * 2 + c},
         ).wait_recv()
 
+    back_copy().start()
+    serve_own(1)
+    remote(
+        qlat.at[:, half_cols(other)],
+        qlat.at[:, half_cols(other)],
+        q_sem.at[2],
+        q_sem.at[3],
+        {"head": sibling},
+    ).wait_recv()
     uq_copy.wait()
     uk_copy.wait()
-    query_norm = norm_rows(qlat[...], q_gain[...], QL).astype(BF16)
+    query_norm = norm_rows(qlat[...], q_gain[...].reshape(1, QL), QL).astype(BF16)
     queries = dot(query_norm, uq_buf[...])
+    serve_own(2)
     parts = []
     ropes = []
     for n in range(NH):
@@ -384,7 +482,10 @@
         ropes.append(rotate_pairs(one, new_cos[...], new_sin[...]).astype(BF16))
     order = rows_by_request(False)
     qmine[...] = dot(order, jnp.concatenate(parts, axis=0)).astype(BF16)
-    qrmine[...] = dot(order, jnp.concatenate(ropes, axis=0)).astype(BF16)
+    rotated = dot(order, jnp.concatenate(ropes, axis=0))
+    qr_dup[...] = rotated.astype(BF16)
+    first_lanes = lax.broadcasted_iota(jnp.int32, (128, 128), 1) < ROPE
+    qrmine[...] = jnp.where(first_lanes, rotated[0:128], rotated[128:256]).astype(BF16)
 
     def y_copies(o):
         to = ((y + o) % NY) * NB + b
@@ -399,12 +500,10 @@
     q_rope[y] = qrmine[...]
 
     serve_near(0)
-    serve_own(1)
-    serve_own(2)
-    serve_far(0)
     serve_own(3)
-
-    s = (dot_t(qmine[...], new_lat[...]) + dot_t(qrmine[...], new_rope[...])) * scale
+    serve_near(1)
+
+    s = (dot_t(qmine[...], new_lat[...]) + dot_t(qr_dup[...], new_rope[...])) * scale
     i = lax.broadcasted_iota(jnp.int32, s.shape, 0)
     j = lax.broadcasted_iota(jnp.int32, s.shape, 1)
     live = ((i >> 3) == (j >> 1)) & ((j & 1) <= (i & 1))
@@ -415,7 +514,8 @@
     new_o[...] = dot(p.astype(BF16), new_lat[...]) / total
     new_lse[...] = jnp.broadcast_to(top + jnp.log(total), new_lse.shape)
 
-    serve_near(1)
+    serve_far(0)
+    serve_near(2)
 
     for o in (1, 3, 2):
         src = (y + NY - o) % NY
@@ -427,10 +527,14 @@
                 y_recv.at[o - 1, n],
                 {"head": src * NB + b},
             ).wait_recv()
-    requests = 32
+    serve_near(3)
     for yb in range(NY):
         qf[:, yb * 8 : (yb + 1) * 8, 0:LAT] = q_lat[yb].astype(F32).reshape(requests, 8, LAT)
-        qf[:, yb * 8 : (yb + 1) * 8, LAT:] = q_rope[yb].astype(F32).reshape(requests, 8, 128)
+        both = q_rope[yb].astype(F32)
+        turned = pltpu.roll(both, 64, 1)
+        rows = slice(yb * 8, (yb + 1) * 8)
+        qf[0:16, rows, LAT:] = jnp.where(first_lanes, both, turned).reshape(16, 8, 128)
+        qf[16:32, rows, LAT:] = jnp.where(first_lanes, turned, both).reshape(16, 8, 128)
     qb[0:requests] = qf[...].astype(BF16)
     qb[requests] = jnp.zeros((32, LAT + 128), BF16)
 
@@ -474,42 +578,52 @@
         for dx in places:
             attend(block_at(dx, core), plane(j))
 
-    def attend_ring(j, core):
-        @pl.loop(0, 2)
-        def _(i):
-            for u in range(2):
-                attend(block_at(2 * i + u, core), plane(j))
-
     for one in own:
         one.wait()
     o_slot[96] = jnp.zeros((32, LAT), BF16)
     m_slot[96] = jnp.full((32, 128), LOW, F32)
     l_slot[96] = jnp.zeros((32, 128), F32)
     attend_own(4, c, 0, 0)
-    serve_near(2)
+    for j in range(4):
+        from_sibling(j, (0,))
+    attend_own(4, other, 0, 0)
     attend_places(0, c, (1, 3))
     serve_far(1)
-    attend_places(0, c, (2,))
     attend_places(1, c, (1, 3))
+    from_sibling(0, (1, 3))
+    attend_places(0, other, (1, 3))
     serve_far(2)
-    from_sibling(0, (0, 1, 2, 3))
-    attend_ring(0, other)
-    serve_near(3)
+    from_sibling(1, (1, 3))
+    attend_places(1, other, (1, 3))
     attend_places(2, c, (1, 3))
-    attend_places(1, c, (2,))
-    from_sibling(1, (0, 1, 2, 3))
-    attend_ring(1, other)
     serve_far(3)
-    attend_places(2, c, (2,))
     attend_places(3, c, (1, 3))
-    from_sibling(2, (0, 1, 2, 3))
-    attend_ring(2, other)
-    attend_places(3, c, (2,))
-    from_sibling(3, (0, 1, 2, 3))
-    attend_ring(3, other)
-
-    @pl.loop(0, requests // 2)
-    def _(pair):
+    for j in (2, 3):
+        from_sibling(j, (1, 3))
+        attend_places(j, other, (1, 3))
+    attend_own(4, c, 2, 0)
+    for j in range(4):
+        from_sibling(j, (2,))
+    attend_own(4, other, 2, 0)
+
+    def o_copy(o, n):
+        ty = (y + o) % NY
+        rows = pl.ds(n * 64, 64)
+        return remote(
+            part.at[ty, rows],
+            o_land.at[o - 1, rows],
+            o_send.at[o - 1, n],
+            o_recv.at[o - 1, n],
+            {"head": ty * NB + b},
+        )
+
+    def s_copy(o):
+        ty = (y + o) % NY
+        return remote(
+            stats.at[ty], s_land.at[o - 1], s_send.at[o - 1], s_recv.at[o - 1], {"head": ty * NB + b}
+        )
+
+    def merge_pair(pair):
         mixes = []
         for u in range(2):
             r = pair * 2 + u
@@ -536,24 +650,19 @@
             both = jnp.concatenate([mixes[0][rows], mixes[1][rows]], axis=0)
             part[yb, pl.ds(pl.multiple_of(pair * 16, 16), 16), :] = both.astype(BF16)
 
-    for yb in range(NY):
-        stats[yb] = jnp.transpose(lse_rows[yb])[0:8, :]
-
-    def o_copies(o):
-        ty = (y + o) % NY
-        return [
-            remote(
-                src.at[ty],
-                dst.at[o - 1],
-                o_send.at[o - 1, i],
-                o_recv.at[o - 1, i],
-                {"head": ty * NB + b},
-            )
-            for i, (src, dst) in enumerate(((part, o_land), (stats, s_land)))
-        ]
-
-    for o in (2, 1, 3):
-        start(o_copies(o))
+    for n in range(4):
+
+        @pl.loop(0, 4)
+        def _(i):
+            merge_pair(n * 4 + i)
+
+        if n == 3:
+            for yb in range(NY):
+                stats[yb] = jnp.transpose(lse_rows[yb])[0:8, :]
+            for o in (2, 1, 3):
+                s_copy(o).start()
+        for o in (2, 1, 3):
+            o_copy(o, n).start()
 
     def column(block):
         t_buf[0:8, :] = block
@@ -563,7 +672,9 @@
     lses = [new_lse[:, 0:1], column(stats[y])]
     mixes = [new_o[...], part[y].astype(F32)]
     for o in (1, 3, 2):
-        wait_recv(o_copies(o))
+        s_copy(o).wait_recv()
+        for n in range(4):
+            o_copy(o, n).wait_recv()
         lses.append(column(s_land[o - 1]))
         mixes.append(o_land[o - 1].astype(F32))
     top = lses[0]
@@ -584,17 +695,15 @@
         ).astype(BF16)
 
     wo_copy.wait()
-    width = out.shape[1]
+    width = out.shape[2]
     span = width * NB
-    chip = y * 4 + x
-
     def pair_copy(ty):
         chips = pl.ds(ty * 4, 4)
         return remote(
             sbuf.at[other, chips], sib_land.at[chips], p_send.at[ty], p_recv.at[ty], {"head": sibling}
         )
 
-    for n in range(NY):
+    for n in (1, 2, 3, 0):
         ty = (y + n) % NY
         cols = pl.ds(pl.multiple_of(ty * span, 128), span)
         piece = dot(vals[...], wbuf[0 : w_o.shape[0], cols])
@@ -626,7 +735,7 @@
         return total + rbuf[src].astype(F32)
 
     result = lax.fori_loop(1, 16, body, tbuf[chip].astype(F32))
-    out[...] = result.astype(BF16)
+    out[...] = result.reshape(out.shape).astype(BF16)
 
     for j in (1, 2, 3):
         wait_send(z_copies(j))
@@ -638,7 +747,9 @@
             wait_send(across(j, dx))
     for o in (1, 2, 3):
         wait_send(y_copies(o))
-        wait_send(o_copies(o))
+        s_copy(o).wait_send()
+        for n in range(4):
+            o_copy(o, n).wait_send()
     for ty in range(NY):
         pair_copy(ty).wait_send()
 
@@ -646,11 +757,14 @@
     def _(o):
         out_copy((chip + o) % 16).wait_send()
 
-    @pl.loop(1, N_HEAD)
+    @pl.loop(1, 16)
     def _(o):
-        to = (h + o) % N_HEAD
+        to = (chip + o) % 16
         share_copy(to).wait_send()
         sum_copy(to).wait_send()
+
+    halves_copy().wait_send()
+    back_copy().wait_send()
 
 
 def spec(space):
@@ -694,12 +808,13 @@
     return owner, listed, send_idx, mine % MAXP
 
 
-def angle_tables(positions):
-    lane = jnp.arange(2 * ROPE, dtype=jnp.int32)
-    inverse_freq = 10000.0 ** (-2.0 * (lane % 32).astype(F32) / ROPE)
-    angles = jnp.repeat(positions.astype(F32), ROPE, axis=1) * inverse_freq[None, :]
-    sign = jnp.where((lane % ROPE) < 32, -1.0, 1.0).astype(F32)
-    return jnp.cos(angles), jnp.sin(angles) * sign[None, :]
+def angle_tables():
+    lane = np.arange(2 * ROPE)
+    inverse_freq = 10000.0 ** (-2.0 * (lane % 32) / ROPE)
+    steps = np.concatenate([np.arange(17) * PAGE, np.arange(2), np.zeros(5)])
+    far = steps[:, None] * inverse_freq[None, :]
+    near = (np.arange(32)[:, None] + 32 * (lane // ROPE)[None, :]) * inverse_freq[None, :]
+    return [jnp.asarray(t, F32) for t in (np.cos(far), np.sin(far), np.cos(near), np.sin(near))]
 
 
 def on_device(
@@ -714,22 +829,13 @@
     owner, listed, send_idx, my_depth = page_plan(
         block_table, ctx_pages, g, y, b, per_rank, pages_dev
     )
-    lengths = lax.dynamic_slice_in_dim(ctx_pages, g * per_rank, per_rank, 0)
-    t = jnp.arange(32, dtype=jnp.int32)
-    page_pos = my_depth[:, None, None] * PAGE + t[None, :, None] + jnp.array([0, 32], jnp.int32)
-    page_cos, page_sin = angle_tables(page_pos.reshape(-1, 2))
-    new_pos = (lengths[:, None] * PAGE + jnp.arange(2, dtype=jnp.int32)[None, :]).reshape(-1, 1)
-    new_cos, new_sin = angle_tables(jnp.concatenate([new_pos, new_pos], axis=1))
-    share = w_dq.shape[0]
-    hpart = lax.dynamic_slice_in_dim(dec_hidden, h * share, share, 2).reshape(-1, share)
-
     dma = pltpu.SemaphoreType.DMA
     width = depth // N_HEAD
     slots = NB * NG * SLOT
     out = pl.pallas_call(
         fused_kernel,
-        out_shape=jax.ShapeDtypeStruct((64, width), BF16),
-        in_specs=[spec(SM)] * 3 + [spec(VM)] * 8 + [spec(ANY)] * 7,
+        out_shape=jax.ShapeDtypeStruct((per_rank, 2, width), BF16),
+        in_specs=[spec(SM)] * 5 + [spec(VM)] * 6 + [spec(ANY)] * 8,
         out_specs=spec(VM),
         scratch_shapes=[
             pltpu.VMEM((tokens + 64, depth), BF16),
@@ -743,12 +849,18 @@
             pltpu.VMEM((pages_dev, 32, 128), BF16),
             pltpu.VMEM((NG, ROWS, LAT), BF16),
             pltpu.VMEM((NG, RROWS, 128), BF16),
+            pltpu.VMEM((384, QL), BF16),
+            pltpu.VMEM((64, 128), F32),
+            pltpu.VMEM((64, 128), F32),
             pltpu.VMEM((64, QL), F32),
-            pltpu.VMEM((N_HEAD, 8, 384), F32),
+            pltpu.VMEM((64, QL // 2), F32),
+            pltpu.VMEM((64, QL // 2), F32),
+            pltpu.VMEM((16, 8, 384), F32),
             pltpu.VMEM((8, 384), F32),
             pltpu.VMEM((64, QL), F32),
             pltpu.VMEM((256, LAT), BF16),
             pltpu.VMEM((256, 128), BF16),
+            pltpu.VMEM((128, 128), BF16),
             pltpu.VMEM((64, LAT), BF16),
             pltpu.VMEM((64, 128), BF16),
             pltpu.VMEM((256, LAT), F32),
@@ -756,7 +868,7 @@
             pltpu.VMEM((NB, NG, ROWS, LAT), BF16),
             pltpu.VMEM((NB, NG, RROWS, 128), BF16),
             pltpu.VMEM((NY, 256, LAT), BF16),
-            pltpu.VMEM((NY, 256, 128), BF16),
+            pltpu.VMEM((NY, 128, 128), BF16),
             pltpu.VMEM((32, 32, LAT + 128), F32),
             pltpu.VMEM((33, 32, LAT + 128), BF16),
             pltpu.VMEM((slots + 1, 32, LAT), BF16),
@@ -773,8 +885,8 @@
             pltpu.VMEM((16, 64, width), BF16),
             pltpu.VMEM((16, 64, width), BF16),
             pltpu.VMEM((16, 64, width), BF16),
-            dma((depth // KCHUNK, 3)),
-            dma((4,)),
+            dma((depth // KCHUNK, 2)),
+            dma((6,)),
             dma((2,)),
             dma((3, 2)),
             dma((3, 2)),
@@ -784,14 +896,17 @@
             dma((4, 2)),
             dma((4, 4, 2)),
             dma((4, 4, 2)),
-            dma((N_HEAD,)),
-            dma((N_HEAD,)),
-            dma((N_HEAD,)),
-            dma((N_HEAD,)),
+            dma((4,)),
+            dma((16,)),
+            dma((16,)),
+            dma((16,)),
+            dma((16,)),
             dma((3, 2)),
             dma((3, 2)),
-            dma((3, 2)),
-            dma((3, 2)),
+            dma((3, 4)),
+            dma((3, 4)),
+            dma((3,)),
+            dma((3,)),
             dma((4,)),
             dma((4,)),
             dma((16,)),
@@ -804,23 +919,21 @@
         send_idx,
         owner,
         listed,
-        hpart,
-        w_dq,
-        kv_gain.reshape(1, -1),
-        q_gain.reshape(1, -1),
-        page_cos,
-        page_sin,
-        new_cos,
-        new_sin,
+        my_depth,
+        ctx_pages,
+        kv_gain,
+        q_gain,
+        *angle_tables(),
         prompt,
         dec_hidden,
+        w_dq,
         w_dkv.T,
         w_uq,
         w_uk,
         w_uv,
         w_o,
     )
-    return out.reshape(per_rank, 2, width)
+    return out
 
 
 def solution(mesh):

time: 112 us -> 98 us (0.88)
  Pallas kernels: 101 us -> 91.7 us
  local copies, waits for them, and re-layouts: 4.77 us -> 2 us
  other arithmetic: 6.24 us -> 4.01 us
    pallas_call x1, Pallas kernels: 101 us -> 91.7 us  [on_device(): pl.pallas_call(fused_kernel, out_shape=jax.ShapeDtypeStruct((per_rank, 2,...]
    reshape x5 -> x0, local copies, waits for them, and re-layouts: 2.85 us -> none  [the longest x1 1.39 us: on_device(): return out.reshape(per_rank, 2, width)]
    mul x4 -> x0, other arithmetic: 2.55 us -> none  [the longest x2 1.81 us: angle_tables(): return (jnp.cos(angles), jnp.sin(angles) * sign[None, :])]
    unnamed x2 -> x1, local copies, waits for them, and re-layouts: 0.01 us -> 1.4 us
where the time goes in v2:
time: 98 us; the launch traced here: 97.7 us
  Pallas kernels  91.7 us (94%)
  other arithmetic  4.01 us (4%)
  local copies, waits for them, and re-layouts  2 us (2%)
    pallas_call x1, Pallas kernels, on_device(): pl.pallas_call(fused_kernel, out_shape=jax.ShapeDtypeStruct((per_rank, 2,...  91.7 us

profile of v2, /device:TPU:1, one launch (start us, length us, event | category | flops | bytes accessed | tf_op | source)
XLA Modules:
  0.0 97.7 jit_solution(8624739422824534689)
XLA Ops:
  0.0 0.7 fusion.3
  0.7 0.1 copy.24
  0.8 0.1 eq.85
  0.9 0.3 select_reduce_fusion
  1.2 0.1 reshape.156
  1.4 0.1 copy.25
  1.5 0.1 convert_reduce_fusion
  1.6 0.3 add_reduce_fusion
  1.9 0.6 select_reduce_fusion.3.send_idx
  2.6 0.1 copy.29
  2.7 0.1 reshape.157
  2.8 0.6 compare_select_fusion.2.owner
  3.4 0.1 select_reduce_fusion.1
  3.5 0.6 broadcast_add_fusion.listed
  4.1 0.6 and_select_fusion.depths
  4.7 91.7 %shard_map.154 = bf16[32,2,224]{2,1,0:T(2,128)(2,1)} custom-call(s32[12]{0:T(128)} %select_reduce_fusion.3.send_idx, s32[96]{0:T(128)} %compare_select_fusion.2.owner, s32[512]{0:T(512)} %broadcast_add_fusion.listed, s32[6]{0:T(128)} %and_select_fusion.depths, s32[128]{0:T(128)} %lengths.1, f32[512]{0:T(512)} %kv_gain.1, f32[1536]{0:T(1024)} %q_gain.1, ...), custom_call_target="tpu_custom_call" | custom-call | tf_op jit(solution)/shard_map/pallas_call | solution.py:835
  96.3 1.4 %copy.31 = bf16[32,2,224]{2,1,0:T(2,128)(2,1)} copy(bf16[32,2,224]{2,1,0:T(2,128)(2,1)} %shard_map.154) | data formatting | bytes 57344
  (7 shorter events, 0.1 us)

commit v3 on v2

--- a/solution.py
+++ b/solution.py
@@ -20,6 +20,7 @@
 N_HEAD = 32
 ROWS = SLOT * PAGE
 RROWS = SLOT * PAGE // 2
+FOUR = 4
 KCHUNK = 1024
 AHEAD = 3
 OFFS = (0, 1, 3, 2)
@@ -361,28 +362,32 @@
             zlat[j, k * PAGE : (k + 1) * PAGE, :] = lat_own[page]
             zrope[j, k * 32 : (k + 1) * 32, :] = rope_own[page]
 
+    def place(ref, at, j):
+        rows = ref.shape[1] // NG
+        return ref.at[at, pl.ds(j * rows, rows)]
+
+    def half_place(ref, at, j, side):
+        rows = ref.shape[1] // NG // 2
+        return ref.at[at, pl.ds((j * 2 + side) * rows, rows)]
+
     def z_copies(j):
         rank = (g + OFFS[j]) % NG
         return [
             remote(
-                src.at[j], dst.at[b, g], z_send.at[j - 1, i], z_recv.at[j - 1, i], {"grp": rank}
+                src.at[j], place(dst, b, j), z_send.at[j - 1, i], z_recv.at[j - 1, i], {"grp": rank}
             )
             for i, (src, dst) in enumerate(((zlat, lat_all), (zrope, rope_all)))
         ]
 
-    def plane(j):
-        return (g + NG - OFFS[j]) % NG
-
     def block_at(dx, core):
         return ((x + dx) % 4) * 2 + core
 
     def ring_copies(j, dx, to, send, recv):
-        gs = plane(j)
         at = block_at(dx, c)
         res = []
         for i, (mine, ref) in enumerate(((zlat, lat_all), (zrope, rope_all))):
-            src = mine.at[0] if (j == 0 and dx == 0) else ref.at[at, gs]
-            res.append(remote(src, ref.at[at, gs], send.at[i], recv.at[i], {"head": to}))
+            src = mine.at[0] if (j == 0 and dx == 0) else place(ref, at, j)
+            res.append(remote(src, place(ref, at, j), send.at[i], recv.at[i], {"head": to}))
         return res
 
     def to_right(j):
@@ -391,20 +396,27 @@
     def to_left(j):
         return ring_copies(j, 0, left, x_send.at[j, 1], x_recv.at[j, 1])
 
-    def onward(j):
-        if j in (0, 3):
-            return ring_copies(j, 3, right, f_send.at[j], f_recv.at[j])
-        return ring_copies(j, 1, left, f_send.at[j], f_recv.at[j])
+    def onward(j, side):
+        at = block_at(1 if side else 3, c)
+        return [
+            remote(
+                half_place(ref, at, j, side),
+                half_place(ref, at, j, side),
+                f_send.at[j, side, i],
+                f_recv.at[j, side, i],
+                {"head": left if side else right},
+            )
+            for i, ref in enumerate((lat_all, rope_all))
+        ]
 
     def across(j, dx):
         return ring_copies(j, dx, sibling, c_send.at[j, dx], c_recv.at[j, dx])
 
     def arrived(j, dx, core, sem):
-        gs = plane(j)
         at = block_at(dx, core)
         for i, ref in enumerate((lat_all, rope_all)):
             remote(
-                ref.at[at, gs], ref.at[at, gs], sem.at[i], sem.at[i], {"head": sibling}
+                place(ref, at, j), place(ref, at, j), sem.at[i], sem.at[i], {"head": sibling}
             ).wait_recv()
 
     def serve_own(j):
@@ -416,16 +428,19 @@
 
     def serve_near(j):
         arrived(j, 3, c, x_recv.at[j, 0])
-        if j in (0, 3):
-            start(onward(j))
+        start(onward(j, 0))
         start(across(j, 3))
         arrived(j, 1, c, x_recv.at[j, 1])
-        if j in (1, 2):
-            start(onward(j))
+        start(onward(j, 1))
         start(across(j, 1))
 
     def serve_far(j):
-        arrived(j, 2, c, f_recv.at[j])
+        at = block_at(2, c)
+        for side in range(2):
+            for i, ref in enumerate((lat_all, rope_all)):
+                there = half_place(ref, at, j, side)
+                sem = f_recv.at[j, side, i]
+                remote(there, there, sem, sem, {"head": sibling}).wait_recv()
         start(across(j, 2))
 
     def from_sibling(j, places):
@@ -435,8 +450,8 @@
     for j in (1, 2, 3):
         start(z_copies(j))
     own = [
-        pltpu.make_async_copy(zlat.at[0], lat_all.at[b, g], own_sem.at[0]),
-        pltpu.make_async_copy(zrope.at[0], rope_all.at[b, g], own_sem.at[1]),
+        pltpu.make_async_copy(zlat.at[0], place(lat_all, b, 0), own_sem.at[0]),
+        pltpu.make_async_copy(zrope.at[0], place(rope_all, b, 0), own_sem.at[1]),
     ]
     start(own)
     serve_own(0)
@@ -527,7 +542,6 @@
                 y_recv.at[o - 1, n],
                 {"head": src * NB + b},
             ).wait_recv()
-    serve_near(3)
     for yb in range(NY):
         qf[:, yb * 8 : (yb + 1) * 8, 0:LAT] = q_lat[yb].astype(F32).reshape(requests, 8, LAT)
         both = q_rope[yb].astype(F32)
@@ -538,73 +552,75 @@
     qb[0:requests] = qf[...].astype(BF16)
     qb[requests] = jnp.zeros((32, LAT + 128), BF16)
 
-    row = lax.broadcasted_iota(jnp.int32, (SLOT * 32, ROWS), 0)
-    col = lax.broadcasted_iota(jnp.int32, (SLOT * 32, ROWS), 1)
+    row = lax.broadcasted_iota(jnp.int32, (FOUR * 32, FOUR * PAGE), 0)
+    col = lax.broadcasted_iota(jnp.int32, (FOUR * 32, FOUR * PAGE), 1)
     own_page = (row >> 5) == (col >> 6)
     low_lane = lax.broadcasted_iota(jnp.int32, (32, 128), 1) < ROPE
 
-    def attend(at, gs):
-        first = (at * NG + gs) * SLOT
-        keys = lat_all[at, gs]
-        pairs = rope_all[at, gs]
+    def attend(at, t):
+        first = at * NG * SLOT + t * FOUR
+        keys = lat_all[at, pl.ds(pl.multiple_of(t * FOUR * PAGE, 256), FOUR * PAGE), :]
+        pairs = rope_all[at, pl.ds(pl.multiple_of(t * FOUR * 32, 128), FOUR * 32), :]
         zero = jnp.zeros((32, 128), BF16)
         ropes = []
-        for k in range(SLOT):
+        for k in range(FOUR):
             pair = pairs[k * 32 : (k + 1) * 32, :]
             ropes += [jnp.where(low_lane, pair, zero), jnp.where(low_lane, zero, pair)]
-        q = jnp.concatenate([qb[owner[first + k]] for k in range(SLOT)], axis=0)
+        q = jnp.concatenate([qb[owner[first + k]] for k in range(FOUR)], axis=0)
         s = dot_t(q[:, 0:LAT], keys) + dot_t(q[:, LAT:], jnp.concatenate(ropes, axis=0))
         s = jnp.where(own_page, s * scale, LOW)
         top = jnp.max(s, axis=1, keepdims=True)
         p = jnp.where(own_page, jnp.exp(s - top), 0.0)
         total = jnp.sum(p, axis=1, keepdims=True)
         o = dot(p.astype(BF16), keys)
-        top = jnp.broadcast_to(top, (SLOT * 32, 128))
-        total = jnp.broadcast_to(total, (SLOT * 32, 128))
-        o_slot[pl.ds(first, SLOT)] = o.astype(BF16).reshape(SLOT, 32, LAT)
-        m_slot[pl.ds(first, SLOT)] = top.reshape(SLOT, 32, 128)
-        l_slot[pl.ds(first, SLOT)] = total.reshape(SLOT, 32, 128)
-
-    def gray(j):
-        return j ^ (j >> 1)
-
-    def attend_own(n, core, dx, j0):
-        @pl.loop(0, n // 2)
-        def _(i):
-            for u in range(2):
-                attend(block_at(dx, core), (g + NG - gray(j0 + 2 * i + u)) % NG)
-
-    def attend_places(j, core, places):
-        for dx in places:
-            attend(block_at(dx, core), plane(j))
+        top = jnp.broadcast_to(top, (FOUR * 32, 128))
+        total = jnp.broadcast_to(total, (FOUR * 32, 128))
+        o_slot[pl.ds(first, FOUR)] = o.astype(BF16).reshape(FOUR, 32, LAT)
+        m_slot[pl.ds(first, FOUR)] = top.reshape(FOUR, 32, 128)
+        l_slot[pl.ds(first, FOUR)] = total.reshape(FOUR, 32, 128)
+
+    def attend_blocks(core, places, first, last):
+        if last - first == 1:
+            for dx in places:
+                attend(block_at(dx, core), first)
+            return
+
+        @pl.loop(first, last)
+        def _(t):
+            for dx in places:
+                attend(block_at(dx, core), t)
 
     for one in own:
         one.wait()
     o_slot[96] = jnp.zeros((32, LAT), BF16)
     m_slot[96] = jnp.full((32, 128), LOW, F32)
     l_slot[96] = jnp.zeros((32, 128), F32)
-    attend_own(4, c, 0, 0)
     for j in range(4):
         from_sibling(j, (0,))
-    attend_own(4, other, 0, 0)
-    attend_places(0, c, (1, 3))
+
+    @pl.loop(0, NG * SLOT // FOUR)
+    def _(t):
+        attend(block_at(0, c), t)
+        attend(block_at(0, other), t)
+
+    serve_near(3)
+    attend_blocks(c, (1, 3), 0, 2)
     serve_far(1)
-    attend_places(1, c, (1, 3))
-    from_sibling(0, (1, 3))
-    attend_places(0, other, (1, 3))
+    for j in range(3):
+        from_sibling(j, (1, 3))
+    attend_blocks(other, (1, 3), 0, 2)
     serve_far(2)
-    from_sibling(1, (1, 3))
-    attend_places(1, other, (1, 3))
-    attend_places(2, c, (1, 3))
+    attend_blocks(c, (1, 3), 2, 3)
+    attend_blocks(c, (2,), 0, 2)
+    from_sibling(3, (1, 3))
     serve_far(3)
-    attend_places(3, c, (1, 3))
-    for j in (2, 3):
-        from_sibling(j, (1, 3))
-        attend_places(j, other, (1, 3))
-    attend_own(4, c, 2, 0)
-    for j in range(4):
+    attend_blocks(other, (1, 3), 2, 3)
+    for j in range(3):
         from_sibling(j, (2,))
-    attend_own(4, other, 2, 0)
+    attend_blocks(other, (2,), 0, 2)
+    attend_blocks(c, (2,), 2, 3)
+    from_sibling(3, (2,))
+    attend_blocks(other, (2,), 2, 3)
 
     def o_copy(o, n):
         ty = (y + o) % NY
@@ -742,7 +758,8 @@
     for j in range(4):
         wait_send(to_right(j))
         wait_send(to_left(j))
-        wait_send(onward(j))
+        wait_send(onward(j, 0))
+        wait_send(onward(j, 1))
         for dx in range(4):
             wait_send(across(j, dx))
     for o in (1, 2, 3):
@@ -780,7 +797,9 @@
     ).reshape(1, -1)
     at = jnp.arange(NG * NB * pages_dev, dtype=jnp.int32)
     per_plane = NB * pages_dev
-    ids = (at // per_plane) * (N_HEAD * pages_dev) + y * per_plane + at % per_plane
+    behind = at // per_plane
+    plane = (g + NG - (behind ^ (behind >> 1))) % NG
+    ids = plane * (N_HEAD * pages_dev) + y * per_plane + at % per_plane
     codes = jnp.arange(flat.shape[1], dtype=jnp.int32)[None, :]
     code = jnp.sum(jnp.where(flat == ids[:, None], codes, 0), axis=1)
     code = code.reshape(NG, NB, pages_dev)
@@ -798,9 +817,9 @@
     total = held.shape[0]
     spare = jnp.arange(total, dtype=jnp.int32) - total
     listed = total + jnp.sum(jnp.where(held[None, :] == wanted[:, None], spare[None, :], 0), axis=1)
-    mine = lax.dynamic_slice(code, (g, b, 0), (1, 1, pages_dev)).reshape(-1)
-    my_target = lax.dynamic_slice(target, (g, b, 0), (1, 1, pages_dev)).reshape(-1)
-    my_slot = lax.dynamic_slice(slot, (g, b, 0), (1, 1, pages_dev)).reshape(-1)
+    mine = lax.dynamic_slice(code, (0, b, 0), (1, 1, pages_dev)).reshape(-1)
+    my_target = lax.dynamic_slice(target, (0, b, 0), (1, 1, pages_dev)).reshape(-1)
+    my_slot = lax.dynamic_slice(slot, (0, b, 0), (1, 1, pages_dev)).reshape(-1)
     sends = (my_target[None, :] * SLOT + my_slot[None, :]) == jnp.arange(
         NG * SLOT, dtype=jnp.int32
     )[:, None]
@@ -865,8 +884,8 @@
             pltpu.VMEM((64, 128), BF16),
             pltpu.VMEM((256, LAT), F32),
             pltpu.VMEM((256, 128), F32),
-            pltpu.VMEM((NB, NG, ROWS, LAT), BF16),
-            pltpu.VMEM((NB, NG, RROWS, 128), BF16),
+            pltpu.VMEM((NB, NG * ROWS, LAT), BF16),
+            pltpu.VMEM((NB, NG * RROWS, 128), BF16),
             pltpu.VMEM((NY, 256, LAT), BF16),
             pltpu.VMEM((NY, 128, 128), BF16),
             pltpu.VMEM((32, 32, LAT + 128), F32),
@@ -892,8 +911,8 @@
             dma((3, 2)),
             dma((4, 2, 2)),
             dma((4, 2, 2)),
-            dma((4, 2)),
-            dma((4, 2)),
+            dma((4, 2, 2)),
+            dma((4, 2, 2)),
             dma((4, 4, 2)),
             dma((4, 4, 2)),
             dma((4,)),

time: 98 us -> 94.5 us (0.964)
  Pallas kernels: 91.7 us -> 88.2 us
    pallas_call x1, Pallas kernels: 91.7 us -> 88.2 us  [on_device(): pl.pallas_call(fused_kernel, out_shape=jax.ShapeDtypeStruct((per_rank, 2,...]
where the time goes in v3:
time: 94.5 us; the launch traced here: 94.3 us
  Pallas kernels  88.2 us (93%)
  other arithmetic  4.01 us (4%)
  local copies, waits for them, and re-layouts  2 us (2%)
    pallas_call x1, Pallas kernels, on_device(): pl.pallas_call(fused_kernel, out_shape=jax.ShapeDtypeStruct((per_rank, 2,...  88.2 us

profile of v3, /device:TPU:1, one launch (start us, length us, event | category | flops | bytes accessed | tf_op | source)
XLA Modules:
  0.0 94.3 jit_solution(5502549808529186143)
XLA Ops:
  0.0 0.7 fusion.3
  0.7 0.1 copy.24
  0.8 0.1 eq.86
  0.9 0.3 select_reduce_fusion
  1.3 0.1 reshape.170
  1.4 0.1 copy.25
  1.5 0.1 convert_reduce_fusion
  1.6 0.3 add_reduce_fusion
  1.9 0.6 select_reduce_fusion.3.send_idx
  2.6 0.1 copy.29
  2.7 0.1 reshape.171
  2.8 0.6 compare_select_fusion.4.owner
  3.4 0.1 select_reduce_fusion.1
  3.5 0.6 broadcast_add_fusion.listed
  4.1 0.6 and_select_fusion.depths
  4.7 88.2 %shard_map.154 = bf16[32,2,224]{2,1,0:T(2,128)(2,1)} custom-call(s32[12]{0:T(128)} %select_reduce_fusion.3.send_idx, s32[96]{0:T(128)} %compare_select_fusion.4.owner, s32[512]{0:T(512)} %broadcast_add_fusion.listed, s32[6]{0:T(128)} %and_select_fusion.depths, s32[128]{0:T(128)} %lengths.1, f32[512]{0:T(512)} %kv_gain.1, f32[1536]{0:T(1024)} %q_gain.1, ...), custom_call_target="tpu_custom_call" | custom-call | tf_op jit(solution)/shard_map/pallas_call | solution.py:854
  92.9 1.4 %copy.31 = bf16[32,2,224]{2,1,0:T(2,128)(2,1)} copy(bf16[32,2,224]{2,1,0:T(2,128)(2,1)} %shard_map.154) | data formatting | bytes 57344
  (7 shorter events, 0.1 us)

commit v4 on v3

--- a/solution.py
+++ b/solution.py
@@ -20,6 +20,10 @@
 N_HEAD = 32
 ROWS = SLOT * PAGE
 RROWS = SLOT * PAGE // 2
+AT_DEPTH = NG * SLOT
+AT_OWNER = 32
+AT_LIST = AT_OWNER + NB * NG * SLOT
+GROUPS = 8
 FOUR = 4
 KCHUNK = 1024
 AHEAD = 3
@@ -57,10 +61,7 @@
 
 
 def fused_kernel(
-    send_idx,
-    owner,
-    listed,
-    depths,
+    plan,
     lengths,
     kv_gain,
     q_gain,
@@ -345,7 +346,7 @@
     page_cos = []
     page_sin = []
     for p in range(pages):
-        far = pl.ds(depths[p], 1)
+        far = pl.ds(plan[AT_DEPTH + p], 1)
         far_cos, far_sin = cos_far[far, :], sin_far[far, :]
         page_cos.append(far_cos * cos_near[...] - far_sin * sin_near[...])
         page_sin.append((far_sin * cos_near[...] + far_cos * sin_near[...]) * sign)
@@ -358,7 +359,7 @@
     for j in range(4):
         rank = (g + OFFS[j]) % NG
         for k in range(SLOT):
-            page = send_idx[rank * SLOT + k]
+            page = plan[rank * SLOT + k]
             zlat[j, k * PAGE : (k + 1) * PAGE, :] = lat_own[page]
             zrope[j, k * 32 : (k + 1) * 32, :] = rope_own[page]
 
@@ -566,7 +567,7 @@
         for k in range(FOUR):
             pair = pairs[k * 32 : (k + 1) * 32, :]
             ropes += [jnp.where(low_lane, pair, zero), jnp.where(low_lane, zero, pair)]
-        q = jnp.concatenate([qb[owner[first + k]] for k in range(FOUR)], axis=0)
+        q = jnp.concatenate([qb[plan[AT_OWNER + first + k]] for k in range(FOUR)], axis=0)
         s = dot_t(q[:, 0:LAT], keys) + dot_t(q[:, LAT:], jnp.concatenate(ropes, axis=0))
         s = jnp.where(own_page, s * scale, LOW)
         top = jnp.max(s, axis=1, keepdims=True)
@@ -624,7 +625,8 @@
 
     def o_copy(o, n):
         ty = (y + o) % NY
-        rows = pl.ds(n * 64, 64)
+        size = 256 // GROUPS
+        rows = pl.ds(pl.multiple_of(n * size, size), size)
         return remote(
             part.at[ty, rows],
             o_land.at[o - 1, rows],
@@ -643,7 +645,7 @@
         mixes = []
         for u in range(2):
             r = pair * 2 + u
-            at = [listed[r * MAXP + k] for k in range(MAXP)]
+            at = [plan[AT_LIST + r * MAXP + k] for k in range(MAXP)]
             tops = [m_slot[one] for one in at]
             top = tops[0]
             for one in tops[1:]:
@@ -666,19 +668,40 @@
             both = jnp.concatenate([mixes[0][rows], mixes[1][rows]], axis=0)
             part[yb, pl.ds(pl.multiple_of(pair * 16, 16), 16), :] = both.astype(BF16)
 
-    for n in range(4):
-
-        @pl.loop(0, 4)
+    @pl.loop(0, GROUPS)
+    def _(n):
+        @pl.loop(0, 16 // GROUPS)
         def _(i):
-            merge_pair(n * 4 + i)
-
-        if n == 3:
-            for yb in range(NY):
-                stats[yb] = jnp.transpose(lse_rows[yb])[0:8, :]
-            for o in (2, 1, 3):
-                s_copy(o).start()
+            merge_pair(n * (16 // GROUPS) + i)
+
         for o in (2, 1, 3):
             o_copy(o, n).start()
+
+    for yb in range(NY):
+        stats[yb] = jnp.transpose(lse_rows[yb])[0:8, :]
+    for o in (2, 1, 3):
+        s_copy(o).start()
+
+    for j in (1, 2, 3):
+        wait_send(z_copies(j))
+    for j in range(4):
+        wait_send(to_right(j))
+        wait_send(to_left(j))
+        wait_send(onward(j, 0))
+        wait_send(onward(j, 1))
+        for dx in range(4):
+            wait_send(across(j, dx))
+    for o in (1, 2, 3):
+        wait_send(y_copies(o))
+
+    @pl.loop(1, 16)
+    def _(o):
+        to = (chip + o) % 16
+        share_copy(to).wait_send()
+        sum_copy(to).wait_send()
+
+    halves_copy().wait_send()
+    back_copy().wait_send()
 
     def column(block):
         t_buf[0:8, :] = block
@@ -689,7 +712,7 @@
     mixes = [new_o[...], part[y].astype(F32)]
     for o in (1, 3, 2):
         s_copy(o).wait_recv()
-        for n in range(4):
+        for n in range(GROUPS):
             o_copy(o, n).wait_recv()
         lses.append(column(s_land[o - 1]))
         mixes.append(o_land[o - 1].astype(F32))
@@ -753,19 +776,9 @@
     result = lax.fori_loop(1, 16, body, tbuf[chip].astype(F32))
     out[...] = result.reshape(out.shape).astype(BF16)
 
-    for j in (1, 2, 3):
-        wait_send(z_copies(j))
-    for j in range(4):
-        wait_send(to_right(j))
-        wait_send(to_left(j))
-        wait_send(onward(j, 0))
-        wait_send(onward(j, 1))
-        for dx in range(4):
-            wait_send(across(j, dx))
     for o in (1, 2, 3):
-        wait_send(y_copies(o))
         s_copy(o).wait_send()
-        for n in range(4):
+        for n in range(GROUPS):
             o_copy(o, n).wait_send()
     for ty in range(NY):
         pair_copy(ty).wait_send()
@@ -773,15 +786,6 @@
     @pl.loop(1, 16)
     def _(o):
         out_copy((chip + o) % 16).wait_send()
-
-    @pl.loop(1, 16)
-    def _(o):
-        to = (chip + o) % 16
-        share_copy(to).wait_send()
-        sum_copy(to).wait_send()
-
-    halves_copy().wait_send()
-    back_copy().wait_send()
 
 
 def spec(space):
@@ -824,7 +828,8 @@
         NG * SLOT, dtype=jnp.int32
     )[:, None]
     send_idx = jnp.sum(jnp.where(sends, within[None, :], 0), axis=1)
-    return owner, listed, send_idx, mine % MAXP
+    spare = jnp.zeros(AT_OWNER - AT_DEPTH - pages_dev, jnp.int32)
+    return jnp.concatenate([send_idx, mine % MAXP, spare, owner, listed])
 
 
 def angle_tables():
@@ -845,7 +850,7 @@
     tokens, depth = prompt.shape
     pages_dev = tokens // PAGE
     per_rank = dec_hidden.shape[0]
-    owner, listed, send_idx, my_depth = page_plan(
+    plan = page_plan(
         block_table, ctx_pages, g, y, b, per_rank, pages_dev
     )
     dma = pltpu.SemaphoreType.DMA
@@ -854,7 +859,7 @@
     out = pl.pallas_call(
         fused_kernel,
         out_shape=jax.ShapeDtypeStruct((per_rank, 2, width), BF16),
-        in_specs=[spec(SM)] * 5 + [spec(VM)] * 6 + [spec(ANY)] * 8,
+        in_specs=[spec(SM)] * 2 + [spec(VM)] * 6 + [spec(ANY)] * 8,
         out_specs=spec(VM),
         scratch_shapes=[
             pltpu.VMEM((tokens + 64, depth), BF16),
@@ -922,8 +927,8 @@
             dma((16,)),
             dma((3, 2)),
             dma((3, 2)),
-            dma((3, 4)),
-            dma((3, 4)),
+            dma((3, GROUPS)),
+            dma((3, GROUPS)),
             dma((3,)),
             dma((3,)),
             dma((4,)),
@@ -935,10 +940,7 @@
             collective_id=0, has_side_effects=True, vmem_limit_bytes=58 * 1024 * 1024
         ),
     )(
-        send_idx,
-        owner,
-        listed,
-        my_depth,
+        plan,
         ctx_pages,
         kv_gain,
         q_gain,

time: 94.5 us -> 92 us (0.974)
  other arithmetic: 4.01 us -> 1.77 us
  Pallas kernels: 88.2 us -> 87.2 us
    pallas_call x1, Pallas kernels: 88.2 us -> 87.2 us  [on_device(): pl.pallas_call(fused_kernel, out_shape=jax.ShapeDtypeStruct((per_rank, 2,...]
where the time goes in v4:
time: 92 us; the launch traced here: 91.7 us
  Pallas kernels  87.2 us (95%)
  local copies, waits for them, and re-layouts  2.67 us (3%)
  other arithmetic  1.77 us (2%)
    pallas_call x1, Pallas kernels, on_device(): pl.pallas_call(fused_kernel, out_shape=jax.ShapeDtypeStruct((per_rank, 2,...  87.2 us

profile of v4, /device:TPU:1, one launch (start us, length us, event | category | flops | bytes accessed | tf_op | source)
XLA Modules:
  0.0 91.7 jit_solution(12994128359537805366)
XLA Ops:
  0.0 0.7 fusion.3
  0.7 0.1 copy.24
  0.8 0.1 eq.86
  0.9 0.3 select_reduce_fusion
  1.3 0.1 reshape.170
  1.4 0.1 copy.25
  1.5 0.1 convert_reduce_fusion
  1.6 0.3 add_reduce_fusion
  1.9 0.1 select_reduce_fusion.3
  2.1 0.1 copy.29
  2.2 0.1 reshape.172
  2.3 0.1 select_reduce_fusion.1
  2.5 0.7 concatenate.3.plan
  3.1 87.2 %shard_map.154 = bf16[32,2,224]{2,1,0:T(2,128)(2,1)} custom-call(s32[640]{0:T(1024)} %concatenate.3.plan, s32[128]{0:T(128)} %lengths.1, f32[512]{0:T(512)} %kv_gain.1, f32[1536]{0:T(1024)} %q_gain.1, f32[24,128]{1,0:T(8,128)} %constant.137.clone.cos_far, f32[24,128]{1,0:T(8,128)} %constant.138.clone.sin_far, f32[32,128]{1,0:T(8,128)} %constant.139.clone.cos_near, ...), custom_call_target="tpu_custom_call" | custom-call | tf_op jit(solution)/shard_map/pallas_call | solution.py:859
  90.3 1.4 %copy.31 = bf16[32,2,224]{2,1,0:T(2,128)(2,1)} copy(bf16[32,2,224]{2,1,0:T(2,128)(2,1)} %shard_map.154) | data formatting | bytes 57344
  (11 shorter events, 0.1 us)

commit v5 on v4

--- a/solution.py
+++ b/solution.py
@@ -330,7 +330,6 @@
             acc[...] = piece
         else:
             acc[...] += piece
-    send_sums()
     wo_copy.start()
 
     pages = tokens // PAGE
@@ -456,6 +455,7 @@
     ]
     start(own)
     serve_own(0)
+    send_sums()
 
     new_lat[...] = norm_rows(acc[tokens : tokens + 64, 0:LAT], kv_gain[...].reshape(1, LAT), LAT).astype(BF16)
     new_r = acc[tokens : tokens + 64, LAT : LAT + ROPE]

time: 92 us -> 90.6 us (0.985)
  Pallas kernels: 87.2 us -> 85.8 us
    pallas_call x1, Pallas kernels: 87.2 us -> 85.8 us  [on_device(): pl.pallas_call(fused_kernel, out_shape=jax.ShapeDtypeStruct((per_rank, 2,...]
where the time goes in v5:
time: 90.6 us; the launch traced here: 90.3 us
  Pallas kernels  85.8 us (95%)
  local copies, waits for them, and re-layouts  2.67 us (3%)
  other arithmetic  1.77 us (2%)
    pallas_call x1, Pallas kernels, on_device(): pl.pallas_call(fused_kernel, out_shape=jax.ShapeDtypeStruct((per_rank, 2,...  85.8 us

profile of v5, /device:TPU:1, one launch (start us, length us, event | category | flops | bytes accessed | tf_op | source)
XLA Modules:
  0.0 90.3 jit_solution(16835230612347003749)
XLA Ops:
  0.0 0.7 fusion.3
  0.7 0.1 copy.24
  0.8 0.1 eq.86
  0.9 0.3 select_reduce_fusion
  1.3 0.1 reshape.170
  1.4 0.1 copy.25
  1.5 0.1 convert_reduce_fusion
  1.6 0.3 add_reduce_fusion
  1.9 0.1 select_reduce_fusion.3
  2.1 0.1 copy.29
  2.2 0.1 reshape.172
  2.3 0.1 select_reduce_fusion.1
  2.5 0.7 concatenate.3.plan
  3.1 85.8 %shard_map.154 = bf16[32,2,224]{2,1,0:T(2,128)(2,1)} custom-call(s32[640]{0:T(1024)} %concatenate.3.plan, s32[128]{0:T(128)} %lengths.1, f32[512]{0:T(512)} %kv_gain.1, f32[1536]{0:T(1024)} %q_gain.1, f32[24,128]{1,0:T(8,128)} %constant.137.clone.cos_far, f32[24,128]{1,0:T(8,128)} %constant.138.clone.sin_far, f32[32,128]{1,0:T(8,128)} %constant.139.clone.cos_near, ...), custom_call_target="tpu_custom_call" | custom-call | tf_op jit(solution)/shard_map/pallas_call | solution.py:859
  88.9 1.4 %copy.31 = bf16[32,2,224]{2,1,0:T(2,128)(2,1)} copy(bf16[32,2,224]{2,1,0:T(2,128)(2,1)} %shard_map.154) | data formatting | bytes 57344
  (11 shorter events, 0.1 us)
